TPU v7x, 256 devices: a whole 4x4x8 slice. The times are simulated.
256 devices in a mesh: dp: 16 (over z, core), expert: 16 (over x, y).
Axes of the slice: x: 4, y: 4, z: 8, core: 2. Of those that a mesh axis runs over, the one named last changes fastest.
Arguments:
- hidden: bfloat16 [36864, 2048], P(('dp', 'expert')), may hold values from -6 to 6
- w_gate: bfloat16 [32, 2048, 384], P('expert'), may hold values from -0.125 to 0.125
- w_up: bfloat16 [32, 2048, 384], P('expert'), may hold values from -0.125 to 0.125
- w_down: bfloat16 [32, 384, 2048], P('expert'), may hold values from -0.3125 to 0.3125
- expert_ids: int32 [36864, 8], P(('dp', 'expert')), may hold values from 0 to 31, as said below
- route_weight: bfloat16 [36864, 8], P(('dp', 'expert')), may hold values from 0.029907227 to 0.29882812
- seq_len: int32 [768], P(('dp', 'expert')), may hold values from 36 to 48, as said below
- positive: int32 [256], P(('dp', 'expert')), may hold values from 0 to 31
Outputs:
- query_loss: float32 [256], P(('dp', 'expert'))
- grad_gate: float32 [32, 2048, 384], P('expert', 'dp')
- grad_up: float32 [32, 2048, 384], P('expert', 'dp')
- grad_down: float32 [32, 384, 2048], P('expert', None, 'dp')
Inputs may be any that keep to these rules, and one draw needn't show every extreme that they name: `expert_ids`: among the valid token slots of one block, no expert is named by more than 38 of them; the ids of slots that are not valid carry no data. `seq_len`: valid tokens of a sequence of 48 slots; some blocks hold only full sequences, and blocks differ in how full their sequences are.
All inputs are finite; a program needn't handle non-finite values.
Results may differ from a plain program's by a relative error of at most 0.03.
Values may be sent and summed in bfloat16 or wider, within the bound.
No kernel may reach another device: no remote copies, remote signals or barrier semaphores. Data moves between devices by JAX's collectives and lax.ppermute only.
A program may use at most 128 MiB of HBM per device.

v0:
```python
import jax
import jax.numpy as jnp
from jax import lax
from jax.sharding import PartitionSpec as P

inv_temp = 20.0
loss_scale = 128.0
norm_eps = 1e-06


def silu_parts(gate_pre):
    sigma = jax.nn.sigmoid(gate_pre)
    return (gate_pre * sigma, sigma * (1.0 + gate_pre * (1.0 - sigma)))


def slot_tables(expert_ids, route_weight, seq_len, experts, capacity):
    tok_count, top_count = expert_ids.shape
    seq_count = seq_len.shape[0]
    length = tok_count // seq_count
    position = jnp.arange(tok_count, dtype=jnp.int32)
    member = position[:, None] // length == jnp.arange(seq_count, dtype=jnp.int32)[None, :]
    bound = jnp.sum(jnp.where(member, seq_len[None, :], 0), axis=1)
    valid = position % length < bound
    member_live = jnp.logical_and(member, valid[:, None])
    inverse = 1.0 / seq_len.astype(jnp.float32)
    pool = jnp.where(member_live, inverse[None, :], 0.0)
    hits = jnp.logical_and(
        expert_ids[:, :, None] == jnp.arange(experts, dtype=jnp.int32)[None, None, :],
        valid[:, None, None],
    )
    flat = hits.reshape(tok_count * top_count, experts).astype(jnp.int32)
    before = jnp.cumsum(flat, axis=0) - flat
    place = jnp.sum(before * flat, axis=1).reshape(tok_count, top_count)
    slot = expert_ids * capacity + place
    pick = jnp.logical_and(
        slot[:, :, None] == jnp.arange(experts * capacity, dtype=jnp.int32)[None, None, :],
        valid[:, None, None],
    )
    dispatch = jnp.sum(pick.astype(jnp.float32), axis=1).astype(jnp.bfloat16)
    combine = jnp.sum(
        jnp.where(pick, route_weight.astype(jnp.float32)[:, :, None], 0.0), axis=1
    ).astype(jnp.bfloat16)
    seq_weight = jnp.einsum(
        "ts,tq->sq", combine.astype(jnp.float32), pool, precision=lax.Precision.HIGHEST
    )
    return (pool, dispatch, combine, seq_weight)


def contrast(query_emb, negatives, positive):
    scores = (
        jnp.einsum("qd,pd->qp", query_emb, negatives, preferred_element_type=jnp.float32) * inv_temp
    )
    total = jnp.log(jnp.sum(jnp.exp(scores), axis=1))
    target = jnp.arange(negatives.shape[0], dtype=jnp.int32)[None, :] == positive[:, None]
    loss = total - jnp.sum(jnp.where(target, scores, 0.0), axis=1)
    coeff = (jnp.exp(scores - total[:, None]) - target.astype(jnp.float32)) * (
        loss_scale * inv_temp
    )
    return (loss, coeff)


def body(hidden, w_gate, w_up, w_down, expert_ids, route_weight, seq_len, positive):
    high = lax.Precision.HIGHEST
    tok_count, width = hidden.shape
    exp_local = w_gate.shape[0]
    groups = lax.axis_size("expert")
    experts = exp_local * groups
    top_count = expert_ids.shape[1]
    capacity = min(tok_count, (tok_count * top_count + experts - 1) // experts + 2)
    qry_count = positive.shape[0]
    pool, dispatch, combine, seq_weight = slot_tables(
        expert_ids, route_weight, seq_len, experts, capacity
    )
    outgoing = jnp.einsum("ts,td->sd", dispatch, hidden, preferred_element_type=jnp.float32)
    outgoing = outgoing.astype(jnp.bfloat16).reshape(experts, capacity, width)
    arrived = lax.all_to_all(outgoing, "expert", split_axis=0, concat_axis=0, tiled=True)
    arrived = arrived.reshape(groups, exp_local, capacity, width)
    gate_pre = jnp.einsum("secd,edf->secf", arrived, w_gate, preferred_element_type=jnp.float32)
    up_pre = jnp.einsum("secd,edf->secf", arrived, w_up, preferred_element_type=jnp.float32)
    act, slope = silu_parts(gate_pre)
    inner = (act * up_pre).astype(jnp.bfloat16)
    out_rows = jnp.einsum(
        "secf,efd->secd", inner, w_down, preferred_element_type=jnp.float32
    ).astype(jnp.bfloat16)
    returned = lax.all_to_all(
        out_rows.reshape(experts, capacity, width),
        "expert",
        split_axis=0,
        concat_axis=0,
        tiled=True,
    )
    mixed = hidden.astype(jnp.float32) + jnp.einsum(
        "ts,sd->td",
        combine,
        returned.reshape(experts * capacity, width),
        preferred_element_type=jnp.float32,
    )
    pooled = jnp.einsum("tq,td->qd", pool, mixed, precision=high)
    scale = lax.rsqrt(jnp.sum(pooled * pooled, axis=1) + norm_eps)
    embed = (pooled * scale[:, None]).astype(jnp.bfloat16)
    query_emb = embed[:qry_count]
    negatives = lax.all_gather(embed[qry_count:], "dp", axis=0, tiled=True)
    loss, coeff = contrast(query_emb, negatives, positive)
    grad_q = jnp.dot(coeff, negatives.astype(jnp.float32), precision=high)
    all_grad = jnp.einsum("qp,qd->pd", coeff, query_emb.astype(jnp.float32), precision=high)
    grad_p = lax.psum_scatter(
        all_grad.astype(jnp.bfloat16), "dp", scatter_dimension=0, tiled=True
    ).astype(jnp.float32)
    grad_e = jnp.concatenate([grad_q, grad_p], axis=0)
    along = jnp.sum(pooled * grad_e, axis=1)
    grad_v = scale[:, None] * grad_e - pooled * (scale * scale * scale * along)[:, None]
    slot_grad = jnp.einsum("sq,qd->sd", seq_weight, grad_v, precision=high).astype(jnp.bfloat16)
    grad_rows = lax.all_to_all(
        slot_grad.reshape(experts, capacity, width),
        "expert",
        split_axis=0,
        concat_axis=0,
        tiled=True,
    )
    grad_rows = grad_rows.reshape(groups, exp_local, capacity, width)
    part_down = jnp.einsum("secf,secd->efd", inner, grad_rows, preferred_element_type=jnp.float32)
    grad_inner = jnp.einsum("secd,efd->secf", grad_rows, w_down, preferred_element_type=jnp.float32)
    grad_gate_pre = (grad_inner * up_pre * slope).astype(jnp.bfloat16)
    grad_up_pre = (grad_inner * act).astype(jnp.bfloat16)
    part_gate = jnp.einsum(
        "secd,secf->edf", arrived, grad_gate_pre, preferred_element_type=jnp.float32
    )
    part_up = jnp.einsum("secd,secf->edf", arrived, grad_up_pre, preferred_element_type=jnp.float32)
    grad_gate, grad_up, grad_down = (
        lax.psum_scatter(
            part_gate.astype(jnp.bfloat16), "dp", scatter_dimension=1, tiled=True
        ).astype(jnp.float32),
        lax.psum_scatter(
            part_up.astype(jnp.bfloat16), "dp", scatter_dimension=1, tiled=True
        ).astype(jnp.float32),
        lax.psum_scatter(
            part_down.astype(jnp.bfloat16), "dp", scatter_dimension=2, tiled=True
        ).astype(jnp.float32),
    )
    return (loss, grad_gate, grad_up, grad_down)


def solution(mesh):
    placed = (
        P(("dp", "expert"), None),
        P("expert", None, None),
        P("expert", None, None),
        P("expert", None, None),
        P(("dp", "expert"), None),
        P(("dp", "expert"), None),
        P(("dp", "expert")),
        P(("dp", "expert")),
    )
    return jax.shard_map(
        body,
        mesh=mesh,
        in_specs=placed,
        out_specs=(
            P(("dp", "expert")),
            P("expert", "dp", None),
            P("expert", "dp", None),
            P("expert", None, "dp"),
        ),
        check_vma=False,
    )
```

profile of v0, /device:TPU:4, one launch (start us, length us, event | category | flops | bytes accessed | tf_op | source)
XLA Modules:
  0.0 643.3 jit_solution(4468676731284272856)
XLA Ops:
  10.2 15.9 %reduce-window.6 = s32[32,9,128]{2,1,0:T(8,128)S(1)} reduce-window(s32[32,9,128]{2,1,0:T(8,128)} %fusion.29, s32[]{:T(128)} %constant.31.clone.1), window={size=1x1x128 pad=0_0x0_0x127_0}, to_apply=%region_1.2 | reduce-window | flops 4681728 | bytes 294916 | tf_op jit(solution)/shard_map/reduce-window
  26.9 1.1 copy.58
  31.8 1.4 copy.62
  33.3 5.0 select_reduce_fusion
  38.3 4.8 convolution_convert_fusion.1
  43.1 7.5 %reshape.149 = bf16[32,38,2048]{2,1,0:T(8,128)(2,1)} reshape(bf16[1216,2048]{1,0:T(8,128)(2,1)} %convolution_convert_fusion.1) | data formatting | bytes 9961472 | tf_op jit(solution)/shard_map/reshape | solution.py:75
  50.6 68.0 %all_to_all.15 = bf16[32,38,2048]{2,1,0:T(8,128)(2,1)S(1)} all-to-all(bf16[32,38,2048]{2,1,0:T(8,128)(2,1)} %reshape.149), channel_id=1, replica_groups=mesh['dp'=16,'expert'=16] {'expert'}, dimensions={0} | all-to-all | bytes 9961472 | tf_op jit(solution)/shard_map/all_to_all | solution.py:76
  118.6 2.9 fusion.7
  122.4 4.3 fusion.18
  126.7 3.1 convert_bitcast_fusion
  129.8 2.7 copy.65
  132.5 6.7 %all-to-all-start.1 = ((bf16[32,38,2048]{2,1,0:T(8,128)(2,1)}), bf16[32,38,2048]{2,1,0:T(8,128)(2,1)}, u32[]{:S(2)}, u32[]{:S(2)}) async-start(bf16[32,38,2048]{2,1,0:T(8,128)(2,1)} %bitcast.127), calls=%async_computation.1 | async-start | bytes 10485760 | tf_op jit(solution)/shard_map/all_to_all | solution.py:85
  141.4 61.7 %all-to-all-done.1 = bf16[32,38,2048]{2,1,0:T(8,128)(2,1)} async-done(((bf16[32,38,2048]{2,1,0:T(8,128)(2,1)}), bf16[32,38,2048]{2,1,0:T(8,128)(2,1)}, u32[]{:S(2)}, u32[]{:S(2)}) %all-to-all-start.1) | async-done | bytes 4980768 | tf_op jit(solution)/shard_map/all_to_all | solution.py:85
  203.1 7.5 %reshape.152 = bf16[1216,2048]{1,0:T(8,128)(2,1)} reshape(bf16[32,38,2048]{2,1,0:T(8,128)(2,1)} %all-to-all-done.1) | data formatting | bytes 9961472 | tf_op jit(solution)/shard_map/reshape | solution.py:95
  210.6 3.5 convolution_add_fusion
  215.1 20.3 %all-gather = bf16[16,2,2048]{2,1,0:T(2,128)(2,1)S(1)} all-gather(bf16[1,2,2048]{2,1,0:T(2,128)(2,1)S(1)} %slice_bitcast_fusion), channel_id=1, replica_groups=mesh['dp'=16,'expert'=16] {'dp'}, dimensions={0}, use_global_device_ids=true | all-gather | bytes 139264 | tf_op jit(solution)/shard_map/all_gather | solution.py:102
  237.9 108.3 %all-reduce.3.cloned.1.call-done = bf16[32,2048]{1,0:T(8,128)(2,1)} async-done(((bf16[32,2048]{1,0:T(8,128)(2,1)}), bf16[32,2048]{1,0:T(8,128)(2,1)}) %all-reduce.3.cloned.1.call-update) | async-done | bytes 131088
  347.1 9.7 %convolution_convert_fusion = bf16[1216,2048]{1,0:T(8,128)(2,1)} fusion(f32[1216,3]{0,1:T(4,128)S(1)} %fusion.30, f32[3,2048]{1,0:T(4,128)S(1)} %get-tuple-element.13, f32[2,2048]{1,0:T(2,128)S(1)} %dynamic-slice_convert_fusion, f32[1,2048]{1,0:T(1,128)S(1)} %fusion.69, f32[3]{0:T(128)S(1)} %fusion.65, f32[3]{0:T(128)S(1)} %add_rsqrt_fusion), kind=kOutput, calls=%fused_computation | convolution fusion | flops 92168192 | bytes 5044504 | tf_op jit(solution)/shard_map/sq,qd->sd/dot_general | solution.py:112
  356.8 7.5 %reshape.154 = bf16[32,38,2048]{2,1,0:T(8,128)(2,1)} reshape(bf16[1216,2048]{1,0:T(8,128)(2,1)} %convolution_convert_fusion) | data formatting | bytes 9961472 | tf_op jit(solution)/shard_map/reshape | solution.py:114
  364.3 67.8 %all_to_all.16 = bf16[32,38,2048]{2,1,0:T(8,128)(2,1)S(1)} all-to-all(bf16[32,38,2048]{2,1,0:T(8,128)(2,1)} %reshape.154), channel_id=1, replica_groups=mesh['dp'=16,'expert'=16] {'expert'}, dimensions={0} | all-to-all | bytes 9961472 | tf_op jit(solution)/shard_map/all_to_all | solution.py:113
  432.1 2.3 copy-done.2
  434.4 4.1 bitcast_convert_fusion
  438.5 8.7 %copy.74 = bf16[2,384,2048]{1,0,2:T(2,128)(2,1)} copy(bf16[2,384,2048]{2,1,0:T(8,128)(2,1)} %bitcast_convert_fusion) | data formatting | bytes 6291456
  447.2 4.1 copy.77
  451.7 8.0 %fusion.17 = (bf16[16,2,38,384]{3,2,0,1:T(8,128)(2,1)S(1)}, bf16[16,2,38,384]{3,2,0,1:T(8,128)(2,1)}) fusion(f32[2,16,38,384]{3,2,1,0:T(8,128)} %copy-done.9, f32[2,16,38,384]{3,2,1,0:T(8,128)} %get-tuple-element.11, bf16[2,384,2048]{2,1,0:T(8,128)(2,1)S(1)} %copy-done, bf16[16,2,38,2048]{3,2,1,0:T(8,128)(2,1)} %bitcast.135), kind=kOutput, calls=%fused_computation.27 | convolution fusion | flops 1918672896 | bytes 13729792 | tf_op jit(solution)/shard_map/secd,efd->secf/dot_general | solution.py:122
  459.6 7.9 %bitcast_convert_fusion.1 = bf16[2,2048,384]{2,1,0:T(8,128)(2,1)} fusion(bf16[16,2,38,2048]{3,2,1,0:T(8,128)(2,1)} %bitcast.132, bf16[16,2,38,384]{3,2,0,1:T(8,128)(2,1)S(1)} %get-tuple-element.8), kind=kOutput, calls=%fused_computation.3 | convolution fusion | flops 1914175488 | bytes 9060352 | tf_op jit(solution)/shard_map/secd,secf->edf/dot_general | solution.py:128
  467.6 8.1 %bitcast_convert_fusion.2 = bf16[2,2048,384]{2,1,0:T(8,128)(2,1)} fusion(bf16[16,2,38,2048]{3,2,1,0:T(8,128)(2,1)} %bitcast.133, bf16[16,2,38,384]{3,2,0,1:T(8,128)(2,1)} %get-tuple-element.9), kind=kOutput, calls=%fused_computation.4 | convolution fusion | flops 1914175488 | bytes 9060352 | tf_op jit(solution)/shard_map/secd,secf->edf/dot_general | solution.py:125
  476.3 33.3 %reduce-scatter.10.cloned.1.call-done = bf16[128,768]{1,0:T(8,128)(2,1)} async-done(((bf16[2048,768]{1,0:T(8,128)(2,1)}), bf16[128,768]{1,0:T(8,128)(2,1)}) %reduce-scatter.10.cloned.1.call-update) | async-done | bytes 196624
  511.6 60.3 %reduce-scatter.8.cloned.1.call-done = bf16[2,128,384]{2,1,0:T(8,128)(2,1)} async-done(((bf16[2,2048,384]{2,1,0:T(8,128)(2,1)}), bf16[2,128,384]{2,1,0:T(8,128)(2,1)}) %reduce-scatter.8.cloned.1.call-update) | async-done | bytes 196624 | tf_op jit(solution)/shard_map/reduce_scatter | solution.py:133
  571.9 1.7 convert_element_type.102
  573.6 60.4 %reduce-scatter.6.cloned.1.call-done = bf16[2,128,384]{2,1,0:T(8,128)(2,1)} async-done(((bf16[2,2048,384]{2,1,0:T(8,128)(2,1)}), bf16[2,128,384]{2,1,0:T(8,128)(2,1)}) %reduce-scatter.6.cloned.1.call-update) | async-done | bytes 196624 | tf_op jit(solution)/shard_map/reduce_scatter | solution.py:130
  634.0 1.7 convert_element_type.99
  (69 shorter events, 15.3 us)
Async XLA Ops:
  7.2 119.5 %copy-start = (bf16[2,384,2048]{2,1,0:T(8,128)(2,1)S(1)}, bf16[2,384,2048]{2,1,0:T(8,128)(2,1)}, u32[]{:S(2)}) copy-start(bf16[2,384,2048]{2,1,0:T(8,128)(2,1)} %param.11) | copy-start | bytes 9437188
  50.6 68.0 %copy-start.4 = (bf16[2,2048,384]{2,1,0:T(8,128)(2,1)S(1)}, bf16[2,2048,384]{2,1,0:T(8,128)(2,1)}, u32[]{:S(2)}) copy-start(bf16[2,2048,384]{2,1,0:T(8,128)(2,1)} %param.9) | copy-start | bytes 9437188
  118.6 3.0 copy-start.1
  118.6 3.8 copy-start.5
  122.4 4.3 copy-start.9
  126.7 3.1 copy-start.7
  132.5 7.4 %copy-start.6 = (u32[256]{0:T(256)S(1)}, u32[256]{0:T(256)}, u32[]{:S(2)}) copy-start(u32[256]{0:T(256)} %constant.50) | copy-start | bytes 3076
  132.5 8.6 %copy-start.3 = (s32[3]{0:T(128)S(1)}, s32[3]{0:T(128)}, u32[]{:S(2)}) copy-start(s32[3]{0:T(128)} %param.14) | copy-start | bytes 40
  132.5 70.6 %all-to-all-start.1 = ((bf16[32,38,2048]{2,1,0:T(8,128)(2,1)}), bf16[32,38,2048]{2,1,0:T(8,128)(2,1)}, u32[]{:S(2)}, u32[]{:S(2)}) async-start(bf16[32,38,2048]{2,1,0:T(8,128)(2,1)} %bitcast.127), calls=%async_computation.1 | async-start | bytes 10485760 | tf_op jit(solution)/shard_map/all_to_all | solution.py:85
  139.2 207.0 %all-reduce.3.cloned.1.call-start = ((), (), s32[]{:S(2)}) async-start(), calls=%async_computation.9 | async-start | bytes 262144
  237.7 272.0 %reduce-scatter.10.cloned.1.call-start = ((), (), s32[]{:S(2)}) async-start(), calls=%async_computation.8 | async-start | bytes 3342336
  364.3 70.1 %copy-start.8 = (bf16[16,2,38,384]{3,2,0,1:T(8,128)(2,1)S(1)}, bf16[16,2,38,384]{3,2,0,1:T(8,128)(2,1)}, u32[]{:S(2)}) copy-start(bf16[16,2,38,384]{3,2,0,1:T(8,128)(2,1)} %copy-done.7) | copy-start | bytes 2801668
  432.1 2.3 copy-start.2
  451.4 120.5 %reduce-scatter.8.cloned.1.call-start = ((), (), s32[]{:S(2)}) async-start(), calls=%async_computation.7 | async-start | bytes 3342336 | tf_op jit(solution)/shard_map/reduce_scatter | solution.py:133
  467.5 166.4 %reduce-scatter.6.cloned.1.call-start = ((), (), s32[]{:S(2)}) async-start(), calls=%async_computation.6 | async-start | bytes 3342336 | tf_op jit(solution)/shard_map/reduce_scatter | solution.py:130
Sparse Core Ops, SparseCore 0:
  237.8 108.3 all-reduce.2
  451.5 58.1 reduce-scatter.9
  512.4 59.4 reduce-scatter.7
  574.5 59.4 reduce-scatter.5
where the time goes:
time: 646 us; the launch traced here: 643 us
  waiting for transfers between devices  324 us (50%)
  blocking collectives  156 us (24%)
  matrix products  58.4 us (9%)
  local copies, waits for them, and re-layouts  48.9 us (8%)
  other arithmetic  31.1 us (5%)
  between operations  17.7 us (3%)
  starting transfers between devices  7.03 us (1%)
    unnamed x6, waiting for transfers between devices  142 us
    all_to_all x1, blocking collectives, body(): lax.all_to_all(outgoing, 'expert', split_axis=0, concat_axis=0, tiled=True)  68 us
    all_to_all x1, blocking collectives, body(): lax.all_to_all(slot_grad.reshape(experts, capacity, width), 'expert', spl...  67.8 us
    all_to_all x1, waiting for transfers between devices, body(): lax.all_to_all(out_rows.reshape(experts, capacity, width), 'expert', spli...  61.7 us
    reduce_scatter x1, waiting for transfers between devices, body(): lax.psum_scatter(part_gate.astype(jnp.bfloat16), 'dp', scatter_dimension=...  60.4 us
    reduce_scatter x1, waiting for transfers between devices, body(): lax.psum_scatter(part_up.astype(jnp.bfloat16), 'dp', scatter_dimension=1,...  60.3 us
    all_gather x1, blocking collectives, body(): negatives = lax.all_gather(embed[qry_count:], 'dp', axis=0, tiled=True)  20.3 us
    unnamed x28, local copies, waits for them, and re-layouts  18.6 us
  transfers between devices with their start and end apart: 5, of which 5 were waited for; matrix products, arithmetic and copies ran while one was open for 4% of the time, Pallas kernels for 0%

commit v1 on v0

v1 whole, which is shorter than its diff:
```python
import functools

import jax
import jax.numpy as jnp
from jax import lax
from jax.experimental import pallas as pl
from jax.experimental.pallas import tpu as pltpu
from jax.sharding import Mesh
from jax.sharding import PartitionSpec as P

inv_temp = 20.0
loss_scale = 128.0
norm_eps = 1e-06

BF = jnp.bfloat16
F32 = jnp.float32
I32 = jnp.int32

PART = 80
WIN = 48
SHIFT = 32
META = 44
SEQ_PAD = 4

NN = (((1,), (0,)), ((), ()))
NT = (((1,), (1,)), ((), ()))
TN = (((0,), (0,)), ((), ()))


def iota(shape, axis):
    return lax.broadcasted_iota(I32, shape, axis)


def mm(a, b, dims=NN):
    return lax.dot_general(a, b, dims, preferred_element_type=F32)


def split2(value):
    high = value.astype(BF)
    return high, (value - high.astype(F32)).astype(BF)


def split3(value):
    high = value.astype(BF)
    rest = value - high.astype(F32)
    mid = rest.astype(BF)
    return high, mid, (rest - mid.astype(F32)).astype(BF)


def window_row(expert, place):
    odd = (expert & 1) == 1
    return jnp.where(odd, jnp.where(place < 32, place + 16, place - 26), place)


def dispatch_kernel(length, rows_step, len_ref, ids_ref, rw_ref, hid_ref, out_ref, sum_ref, slot_ref, meta_ref):
    top, tok = ids_ref.shape
    experts = meta_ref.shape[0] // 2
    step = pl.program_id(0)

    @pl.when(step == 0)
    def _():
        pos = iota((1, tok), 1)
        seq = jnp.zeros((1, tok), I32)
        bound = jnp.full((1, tok), len_ref[0], I32)
        for s in range(1, len_ref.shape[0]):
            later = pos >= s * length
            seq = seq + later.astype(I32)
            bound = jnp.where(later, len_ref[s], bound)
        valid = pos - seq * length < bound
        ids = jnp.where(valid, ids_ref[...], -1)
        names = iota((experts, tok), 0)
        hits = [(ids[k : k + 1] == names).astype(F32) for k in range(top)]
        count = functools.reduce(jnp.add, hits)
        earlier = (iota((tok, tok), 0) < iota((tok, tok), 1)).astype(BF)
        before = mm(count.astype(BF), earlier)
        weight = rw_ref[...].astype(F32)
        lane = iota((128, tok), 0)
        marks = (seq + 1).astype(F32)
        meta = jnp.zeros((2 * experts, 128), F32)
        for k in range(top):
            place = jnp.sum(hits[k] * before, axis=0, keepdims=True).astype(I32)
            for m in range(k):
                place = place + (ids[m : m + 1] == ids[k : k + 1]).astype(I32)
            expert = ids[k : k + 1]
            spot = window_row(expert, place)
            where = (expert >> 1) * PART + (expert & 1) * SHIFT + spot
            slot_ref[k : k + 1, :] = jnp.where(valid, where, -1)
            chosen = (lane == spot).astype(BF)
            both = jnp.concatenate([hits[k] * weight[k : k + 1], hits[k] * marks], axis=0)
            meta = meta + mm(both.astype(BF), chosen, NT)
        meta_ref[...] = meta.astype(BF)
        member = jnp.logical_and(iota((8, tok), 0) == seq, valid).astype(BF)
        sum_ref[...] = mm(member, hid_ref[...])

    row = iota((rows_step, tok), 0) + step * rows_step
    picked = row == slot_ref[0:1, :]
    for k in range(1, top):
        picked = jnp.logical_or(picked, row == slot_ref[k : k + 1, :])
    out = mm(picked.astype(BF), hid_ref[...])
    line = iota((rows_step, 2 * experts), 0) + step * rows_step
    col = iota((rows_step, 2 * experts), 1)
    mark = (col >= experts).astype(I32)
    expert = col - experts * mark
    target = (expert >> 1) * PART + META + 2 * (expert & 1) + mark
    extra = mm((line == target).astype(BF), meta_ref[...])
    out_ref[:, 128:] = out[:, 128:].astype(BF)
    out_ref[:, :128] = (out[:, :128] + extra).astype(BF)


def forward_kernel(groups, seqs, arr_ref, gate_ref, up_ref, down_ref, part_ref, a_ref, keep_ref, w_ref, acc_ref):
    width = arr_ref.shape[2]
    e = pl.program_id(0)
    rows = groups * WIN
    quads = groups * SEQ_PAD

    def run(h):
        x = arr_ref[:, h * SHIFT : h * SHIFT + WIN, :].reshape(rows, width)
        gate = mm(x, gate_ref[0])
        up = mm(x, up_ref[0])
        sigma = jax.nn.sigmoid(gate)
        act = gate * sigma
        slope = sigma * (1.0 + gate * (1.0 - sigma))
        ff = gate.shape[1]
        keep_ref[0, :, 0:ff] = (up * slope).astype(BF)
        keep_ref[0, :, ff : 2 * ff] = act.astype(BF)
        inner = (act * up).astype(BF)
        tail = arr_ref[:, 32:48, 0:128].astype(F32)
        at = META - 32 + 2 * h
        wrow = tail[:, at, :].astype(BF)
        srow = tail[:, at + 1, :].astype(BF)
        owner = (iota((quads, groups), 0) >> 2 == iota((quads, groups), 1)).astype(BF)
        wrep = mm(owner, wrow)
        srep = mm(owner, srow)
        number = ((iota((quads, 128), 0) & 3) + 1).astype(F32)
        picked = jnp.where(srep == number, wrep, 0.0).astype(BF)
        spread = jnp.zeros((128, rows), jnp.bool_)
        line, col = iota((128, rows), 0), iota((128, rows), 1)
        for g in range(groups):
            spread = jnp.logical_or(spread, col == line + g * WIN)
        spread = jnp.logical_and(spread, line < WIN).astype(BF)
        block = iota((quads, rows), 0) >> 2
        start = block * WIN
        col = iota((quads, rows), 1)
        inside = jnp.logical_and(col >= start, col < start + WIN)
        weights = jnp.where(inside, mm(picked, spread), 0.0).astype(BF)
        w_ref[0] = weights
        a = mm(weights, inner)
        high, low = split2(a)
        a_ref[...] = high
        both = mm(jnp.concatenate([high, low], axis=0), down_ref[0])
        total = both[:quads] + both[quads:]
        if h == 0:
            acc_ref[...] = total
        else:
            total = total + acc_ref[...]
            for g in range(groups):
                part_ref[g] = total[g * SEQ_PAD : g * SEQ_PAD + SEQ_PAD]

    @pl.when(e == 0)
    def _():
        run(0)

    @pl.when(e == 1)
    def _():
        run(1)


def pool_kernel(len_ref, pos_ref, recv_ref, sum_ref, out_ref):
    groups = recv_ref.shape[0]
    width = recv_ref.shape[2]
    total = sum_ref[0:SEQ_PAD, :]
    for g in range(groups):
        total = total + recv_ref[g]
    row, col = iota((SEQ_PAD, width), 0), iota((SEQ_PAD, width), 1)
    inverse = jnp.zeros((SEQ_PAD, width), F32)
    count = len_ref.shape[0]
    positive = pos_ref[0]
    target = (positive >> 1) * SEQ_PAD + 1 + (positive & 1)
    note = jnp.where(col == 0, target, 0)
    for s in range(count):
        inverse = jnp.where(row == s, 1.0 / jnp.full((SEQ_PAD, width), len_ref[s], I32).astype(F32), inverse)
        note = jnp.where(col == 1 + s, len_ref[s], note)
    value = jnp.where(row == count, note.astype(F32), total * inverse)
    for g in range(groups):
        out_ref[g] = value


def contrast_kernel(at_ref, recv_ref, loss_ref, own_ref, slice_ref, all_ref, grad_ref):
    groups = recv_ref.shape[0]
    width = recv_ref.shape[2]
    quads = groups * SEQ_PAD
    me = at_ref[0]
    for g in range(groups):
        all_ref[g * SEQ_PAD : (g + 1) * SEQ_PAD, :] = recv_ref[g]
    raw = all_ref[...]
    row = iota((quads, 1), 0)
    kind = row & 3
    pooled = jnp.where(kind == 3, 0.0, raw)
    scale = lax.rsqrt(jnp.sum(pooled * pooled, axis=1, keepdims=True) + norm_eps)
    embed = (pooled * scale).astype(BF)
    notes = raw[:, 0:128].astype(BF)
    shift = (iota((quads, quads), 1) == (iota((quads, quads), 0) | 3)).astype(BF)
    notes = mm(shift, jnp.where(iota((quads, 128), 0) & 3 == 3, notes.astype(F32), 0.0).astype(BF))
    lane = iota((quads, 128), 1)
    target = jnp.sum(jnp.where(lane == 0, notes, 0.0), axis=1, keepdims=True)
    length = jnp.sum(jnp.where(lane == 1 + (iota((quads, 128), 0) & 3), notes, 0.0), axis=1, keepdims=True)
    inverse = jnp.where(kind == 3, 0.0, 1.0 / jnp.where(kind == 3, 1.0, length))
    scores = mm(embed, embed, NT) * inv_temp
    col = iota((quads, quads), 1)
    passage = jnp.logical_or((col & 3) == 1, (col & 3) == 2)
    total = jnp.log(jnp.sum(jnp.where(passage, jnp.exp(scores), 0.0), axis=1, keepdims=True))
    hit = (col.astype(F32) == target).astype(F32)
    losses = total - jnp.sum(hit * scores, axis=1, keepdims=True)
    wanted = iota((quads, 128), 0) == me * SEQ_PAD
    loss_ref[...] = jnp.sum(jnp.where(wanted, losses, 0.0), axis=0, keepdims=True)
    coeff = (jnp.where(passage, jnp.exp(scores - total), 0.0) - hit) * (loss_scale * inv_temp)
    coeff = jnp.where(iota((quads, quads), 0) & 3 == 0, coeff, 0.0)
    coeff = coeff + coeff.T
    three = mm(jnp.concatenate(split3(coeff), axis=0), embed)
    grad = three[:quads] + three[quads : 2 * quads] + three[2 * quads :]
    along = jnp.sum(pooled * grad, axis=1, keepdims=True)
    grad = scale * grad - pooled * (scale * scale * scale * along)
    grad = grad * inverse
    for g in range(groups):
        grad_ref[g] = grad[g * SEQ_PAD : (g + 1) * SEQ_PAD]
    own_ref[...] = grad_ref[me]
    slice_ref[...] = grad_ref[:, :, pl.ds(pl.multiple_of(me * 128, 128), 128)]


def backward_kernel(groups, cols, grad_ref, keep_ref, w_ref, down_ref, arr_ref, out_ref, pre_ref):
    local = keep_ref.shape[0]
    rows = groups * WIN
    ff = down_ref.shape[1]

    @pl.when(pl.program_id(0) == 0)
    def _():
        grad = grad_ref[...]
        for e in range(local):
            back = mm(grad, down_ref[e], NT)
            high, low = split2(back)
            two = jnp.concatenate([high, low], axis=0)
            weights = w_ref[e]
            inner = mm(jnp.concatenate([weights, weights], axis=0), two, TN)
            pre_ref[e, :, 0:ff] = (inner * keep_ref[e, :, 0:ff].astype(F32)).astype(BF)
            pre_ref[e, :, ff : 2 * ff] = (inner * keep_ref[e, :, ff : 2 * ff].astype(F32)).astype(BF)

    for e in range(local):
        x = arr_ref[:, e * SHIFT : e * SHIFT + WIN, :].reshape(rows, cols)
        part = mm(x, pre_ref[e], TN).astype(BF)
        for c in range(cols // 128):
            out_ref[c, e] = part[c * 128 : (c + 1) * 128]


def body(hidden, w_gate, w_up, w_down, expert_ids, route_weight, seq_len, positive):
    dp, ep = ("z", "core"), ("x", "y")
    tok, width = hidden.shape
    local, _, ff = w_gate.shape
    groups = lax.axis_size(ep)
    members = lax.axis_size(dp)
    experts = local * groups
    seqs = seq_len.shape[0]
    top = expert_ids.shape[1]
    length = tok // seqs
    quads = groups * SEQ_PAD
    rows = groups * WIN
    me = lax.axis_index(dp).astype(I32).reshape(1)
    smem = pl.BlockSpec(memory_space=pltpu.SMEM)
    big = pltpu.CompilerParams(vmem_limit_bytes=50 * 1024 * 1024)

    steps = 8
    rows_step = groups * PART // steps
    outgoing, hidden_sum = pl.pallas_call(
        functools.partial(dispatch_kernel, length, rows_step),
        grid=(steps,),
        out_shape=(
            jax.ShapeDtypeStruct((groups * PART, width), BF),
            jax.ShapeDtypeStruct((8, width), F32),
        ),
        in_specs=[
            smem,
            pl.BlockSpec((top, tok), lambda i: (0, 0)),
            pl.BlockSpec((top, tok), lambda i: (0, 0)),
            pl.BlockSpec((tok, width), lambda i: (0, 0)),
        ],
        out_specs=(
            pl.BlockSpec((rows_step, width), lambda i: (i, 0)),
            pl.BlockSpec((8, width), lambda i: (0, 0)),
        ),
        scratch_shapes=[pltpu.VMEM((top, tok), I32), pltpu.VMEM((2 * experts, 128), BF)],
        compiler_params=big,
        name="dispatch",
    )(seq_len, expert_ids.T, route_weight.T, hidden)

    arrived = lax.all_to_all(
        outgoing.reshape(groups, PART, width), ep, split_axis=0, concat_axis=0, tiled=True
    )

    partial, summed, keep, weights = pl.pallas_call(
        functools.partial(forward_kernel, groups, seqs),
        grid=(local,),
        out_shape=(
            jax.ShapeDtypeStruct((groups, SEQ_PAD, width), F32),
            jax.ShapeDtypeStruct((quads, local * ff), BF),
            jax.ShapeDtypeStruct((local, rows, 2 * ff), BF),
            jax.ShapeDtypeStruct((local, quads, rows), BF),
        ),
        in_specs=[
            pl.BlockSpec((groups, PART, width), lambda e: (0, 0, 0)),
            pl.BlockSpec((1, width, ff), lambda e: (e, 0, 0)),
            pl.BlockSpec((1, width, ff), lambda e: (e, 0, 0)),
            pl.BlockSpec((1, ff, width), lambda e: (e, 0, 0)),
        ],
        out_specs=(
            pl.BlockSpec((groups, SEQ_PAD, width), lambda e: (0, 0, 0)),
            pl.BlockSpec((quads, ff), lambda e: (0, e)),
            pl.BlockSpec((1, rows, 2 * ff), lambda e: (e, 0, 0)),
            pl.BlockSpec((1, quads, rows), lambda e: (e, 0, 0)),
        ),
        scratch_shapes=[pltpu.VMEM((quads, width), F32)],
        compiler_params=big,
        name="forward",
    )(arrived, w_gate, w_up, w_down)

    all_summed = lax.all_gather(summed, dp, axis=0, tiled=True)
    returned = lax.all_to_all(partial, ep, split_axis=0, concat_axis=0, tiled=True)

    vmem = pl.BlockSpec(memory_space=pltpu.VMEM)
    pooled = pl.pallas_call(
        pool_kernel,
        out_shape=jax.ShapeDtypeStruct((members, SEQ_PAD, width), F32),
        in_specs=[smem, smem, vmem, vmem],
        out_specs=vmem,
        compiler_params=big,
        name="pool",
    )(seq_len, positive, returned, hidden_sum)
    column = lax.all_to_all(pooled, dp, split_axis=0, concat_axis=0, tiled=True)

    loss, own, slices = pl.pallas_call(
        contrast_kernel,
        out_shape=(
            jax.ShapeDtypeStruct((1, 128), F32),
            jax.ShapeDtypeStruct((SEQ_PAD, width), F32),
            jax.ShapeDtypeStruct((members, SEQ_PAD, 128), F32),
        ),
        in_specs=[smem, vmem],
        out_specs=(vmem, vmem, vmem),
        scratch_shapes=[
            pltpu.VMEM((members * SEQ_PAD, width), F32),
            pltpu.VMEM((members, SEQ_PAD, width), F32),
        ],
        compiler_params=big,
        name="contrast",
    )(me, column)
    note = jnp.concatenate(
        [own.astype(BF).reshape(-1, 128), slices.astype(BF).reshape(-1, 128)], axis=0
    )
    spread = lax.all_to_all(
        jnp.broadcast_to(note[None], (groups,) + note.shape), ep, split_axis=0, concat_axis=0, tiled=True
    )
    half = SEQ_PAD * width // 128
    grads = spread[:, :half].reshape(quads, width)
    columns = spread[:, half:].reshape(groups, members, SEQ_PAD, 128)
    columns = jnp.transpose(columns, (1, 0, 2, 3)).reshape(members * quads, 128)

    cols = 256
    shards = width // 128
    partials = pl.pallas_call(
        functools.partial(backward_kernel, groups, cols),
        grid=(width // cols,),
        out_shape=jax.ShapeDtypeStruct((shards, local, 128, 2 * ff), BF),
        in_specs=[
            pl.BlockSpec((quads, width), lambda i: (0, 0)),
            pl.BlockSpec((local, rows, 2 * ff), lambda i: (0, 0, 0)),
            pl.BlockSpec((local, quads, rows), lambda i: (0, 0, 0)),
            pl.BlockSpec((local, ff, width), lambda i: (0, 0, 0)),
            pl.BlockSpec((groups, PART, cols), lambda i: (0, 0, i)),
        ],
        out_specs=pl.BlockSpec((cols // 128, local, 128, 2 * ff), lambda i: (i, 0, 0, 0)),
        scratch_shapes=[pltpu.VMEM((local, rows, 2 * ff), BF)],
        compiler_params=big,
        name="backward",
    )(grads, keep, weights, w_down, arrived)
    reduced = lax.psum_scatter(
        partials.reshape(shards * local * 128, 2 * ff), dp, scatter_dimension=0, tiled=True
    ).reshape(local, 128, 2 * ff)
    grad_down = jnp.einsum(
        "qef,qd->efd",
        all_summed.reshape(members * quads, local, ff),
        columns,
        preferred_element_type=F32,
    )
    return (
        loss[0, :1],
        reduced[:, :, :ff].astype(F32),
        reduced[:, :, ff:].astype(F32),
        grad_down,
    )


def solution(mesh):
    mesh = Mesh(mesh.devices.reshape(8, 2, 4, 4), ("z", "core", "x", "y"))
    dp, ep = ("z", "core"), ("x", "y")
    tokens = P(dp + ep)
    placed = (
        P(dp + ep, None),
        P(ep, None, None),
        P(ep, None, None),
        P(ep, None, None),
        P(dp + ep, None),
        P(dp + ep, None),
        tokens,
        tokens,
    )
    return jax.shard_map(
        body,
        mesh=mesh,
        in_specs=placed,
        out_specs=(tokens, P(ep, dp, None), P(ep, dp, None), P(ep, None, dp)),
        check_vma=False,
    )
```

time: 646 us -> 245 us (0.38)
  waiting for transfers between devices: 324 us -> 85.5 us
  blocking collectives: 156 us -> 84.3 us
  matrix products: 58.4 us -> 1.32 us
  local copies, waits for them, and re-layouts: 48.9 us -> 5.19 us
  Pallas kernels: 0 us -> 36.6 us
  other arithmetic: 31.1 us -> 1.97 us
  starting transfers between devices: 7.03 us -> 14.7 us
    unnamed x6 -> x2, waiting for transfers between devices: 142 us -> 0.03 us
    reduce_scatter x2 -> x1, waiting for transfers between devices: 121 us -> 60.1 us  [body(): lax.psum_scatter(partials.reshape(shards * local * 128, 2 * ff), dp, scat...]
    dot_general x14 -> x1, matrix products: 58.4 us -> 1.32 us  [body(): jnp.einsum('qef,qd->efd', all_summed.reshape(members * quads, local, ff),...]
    all_to_all x2, blocking collectives: 136 us -> 84.3 us  [the longest x1 67.8 us: body(): lax.all_to_all(outgoing.reshape(groups, PART, width), ep, split_axis=0, c...]
    pallas_call x0 -> x5, Pallas kernels: none -> 36.6 us  [the longest x1 13.7 us: body(): pl.pallas_call(functools.partial(forward_kernel, groups, seqs), grid=(loc...]
    all_to_all x1 -> x2, waiting for transfers between devices: 61.7 us -> 25.4 us  [the longest x1 18.1 us: body(): column = lax.all_to_all(pooled, dp, split_axis=0, concat_axis=0, tiled=True)]
    reshape x5 -> x4, local copies, waits for them, and re-layouts: 22.6 us -> 1.96 us  [the longest x1 1.71 us: body(): all_summed.reshape(members * quads, local, ff)]
    all_gather x1 -> x0, blocking collectives: 20.3 us -> none  [body(): negatives = lax.all_gather(embed[qry_count:], 'dp', axis=0, tiled=True)]
  transfers between devices with their start and end apart: 5 -> 4, of which waited for: 5 -> 3; matrix products, arithmetic and copies ran while one was open for 4% -> 1% of each run, Pallas kernels for 0% -> 7%
where the time goes in v1:
time: 245 us; the launch traced here: 244 us
  waiting for transfers between devices  85.5 us (35%)
  blocking collectives  84.3 us (34%)
  Pallas kernels  36.6 us (15%)
  between operations  14.8 us (6%)
  starting transfers between devices  14.7 us (6%)
  local copies, waits for them, and re-layouts  5.19 us (2%)
    all_to_all x1, blocking collectives, body(): lax.all_to_all(outgoing.reshape(groups, PART, width), ep, split_axis=0, c...  67.8 us
    reduce_scatter x1, waiting for transfers between devices, body(): lax.psum_scatter(partials.reshape(shards * local * 128, 2 * ff), dp, scat...  60.1 us
    all_to_all x1, waiting for transfers between devices, body(): column = lax.all_to_all(pooled, dp, split_axis=0, concat_axis=0, tiled=True)  18.1 us
    all_to_all x1, blocking collectives, body(): lax.all_to_all(jnp.broadcast_to(note[None], (groups,) + note.shape), ep,...  16.5 us
    pallas_call x1, Pallas kernels, body(): pl.pallas_call(functools.partial(forward_kernel, groups, seqs), grid=(loc...  13.7 us
    pallas_call x1, Pallas kernels, body(): pl.pallas_call(functools.partial(backward_kernel, groups, cols), grid=(wi...  13.5 us
    all_to_all x1, starting transfers between devices, body(): column = lax.all_to_all(pooled, dp, split_axis=0, concat_axis=0, tiled=True)  8.6 us
    all_to_all x1, waiting for transfers between devices, body(): lax.all_to_all(partial, ep, split_axis=0, concat_axis=0, tiled=True)  7.28 us
  transfers between devices with their start and end apart: 4, of which 3 were waited for; matrix products, arithmetic and copies ran while one was open for 1% of the time, Pallas kernels for 7%

profile of v1, /device:TPU:4, one launch (start us, length us, event | category | flops | bytes accessed | tf_op | source)
XLA Modules:
  0.0 244.4 jit_solution(14190089094645545083)
XLA Ops:
  7.2 0.0 all-gather.2.cloned.1.call-start
  7.2 0.0 copy-start
  7.2 1.1 copy-done
  8.3 0.0 copy-start.1
  8.3 0.7 copy-done.1
  9.0 0.0 copy-start.2
  9.0 0.7 copy-done.2
  9.7 0.0 copy-start.3
  9.7 0.7 copy-done.3
  10.3 6.8 %dispatch.1 = (bf16[1280,2048]{1,0:T(8,128)(2,1)}, f32[8,2048]{1,0:T(8,128)S(1)}) custom-call(s32[3]{0:T(128)S(1)} %copy-done.3, s32[8,144]{1,0:T(8,128)S(1)} %bitcast.18, bf16[8,144]{1,0:T(8,128)(2,1)S(1)} %bitcast.19, bf16[144,2048]{1,0:T(8,128)(2,1)S(1)} %copy-done), custom_call_target="tpu_custom_call" | custom-call | tf_op jit(solution)/shard_map/dispatch/pallas_call | solution.py:272
  17.1 67.8 %all_to_all.20.arr_ref = bf16[16,80,2048]{2,1,0:T(8,128)(2,1)} all-to-all(bf16[16,80,2048]{2,1,0:T(8,128)(2,1)} %bitcast.22), channel_id=1, replica_groups=mesh['z'=8,'core'=2,'x'=4,'y'=4] {'x','y'}, dimensions={0} | all-to-all | bytes 10485760 | tf_op jit(solution)/shard_map/all_to_all | solution.py:294
  84.9 13.7 %forward.1 = (f32[16,4,2048]{2,1,0:T(4,128)}, bf16[64,768]{1,0:T(8,128)(2,1)}, bf16[2,768,768]{2,1,0:T(8,128)(2,1)S(1)}, bf16[2,64,768]{2,1,0:T(8,128)(2,1)S(1)}) custom-call(bf16[16,80,2048]{2,1,0:T(8,128)(2,1)} %all_to_all.20.arr_ref, bf16[2,2048,384]{2,1,0:T(8,128)(2,1)} %gate_ref.1, bf16[2,2048,384]{2,1,0:T(8,128)(2,1)} %up_ref.1, ...), custom_call_target="tpu_custom_call" | custom-call | tf_op jit(solution)/shard_map/forward/pallas_call | solution.py:298
  98.6 0.0 all-gather.2.cloned.1.call-update
  98.6 6.1 %all-to-all-start.1 = ((f32[16,4,2048]{2,1,0:T(4,128)}), f32[16,4,2048]{2,1,0:T(4,128)S(1)}, u32[]{:S(2)}, u32[]{:S(2)}) async-start(f32[16,4,2048]{2,1,0:T(4,128)} %get-tuple-element.14), calls=%async_computation.1 | async-start | bytes 1048576 | tf_op jit(solution)/shard_map/all_to_all | solution.py:325
  105.3 7.3 %all-to-all-done.1.recv_ref = f32[16,4,2048]{2,1,0:T(4,128)S(1)} async-done(((f32[16,4,2048]{2,1,0:T(4,128)}), f32[16,4,2048]{2,1,0:T(4,128)S(1)}, u32[]{:S(2)}, u32[]{:S(2)}) %all-to-all-start.1) | async-done | bytes 524320 | tf_op jit(solution)/shard_map/all_to_all | solution.py:325
  112.6 0.0 copy-done.4
  112.6 1.4 pool.1
  114.0 8.6 %all-to-all-start.2 = ((f32[16,4,2048]{2,1,0:T(4,128)}), f32[16,4,2048]{2,1,0:T(4,128)S(1)}, u32[]{:S(2)}, u32[]{:S(2)}) async-start(f32[16,4,2048]{2,1,0:T(4,128)} %pool.1), calls=%async_computation.2 | async-start | bytes 1048576 | tf_op jit(solution)/shard_map/all_to_all | solution.py:336
  122.6 0.0 reduce-scatter.2.cloned.1.call-start
  122.7 18.1 %all-to-all-done.2.recv_ref = f32[16,4,2048]{2,1,0:T(4,128)S(1)} async-done(((f32[16,4,2048]{2,1,0:T(4,128)}), f32[16,4,2048]{2,1,0:T(4,128)S(1)}, u32[]{:S(2)}, u32[]{:S(2)}) %all-to-all-start.2) | async-done | bytes 524320 | tf_op jit(solution)/shard_map/all_to_all | solution.py:336
  140.8 1.2 contrast.1
  142.1 0.1 broadcast_in_dim.2
  142.2 16.5 %all_to_all.21 = bf16[16,128,128]{2,1,0:T(8,128)(2,1)S(1)} all-to-all(bf16[16,128,128]{2,1,0:T(8,128)(2,1)S(1)} %broadcast_in_dim.2), channel_id=1, replica_groups=mesh['z'=8,'core'=2,'x'=4,'y'=4] {'x','y'}, dimensions={0} | all-to-all | bytes 1048576 | tf_op jit(solution)/shard_map/all_to_all | solution.py:357
  158.7 0.1 reshape.43.grad_ref
  158.8 13.5 %backward.1 = bf16[16,2,128,768]{3,2,1,0:T(8,128)(2,1)} custom-call(bf16[64,2048]{1,0:T(8,128)(2,1)S(1)} %reshape.43.grad_ref, bf16[2,768,768]{2,1,0:T(8,128)(2,1)S(1)} %get-tuple-element.19.keep_ref, bf16[2,64,768]{2,1,0:T(8,128)(2,1)S(1)} %get-tuple-element.20.w_ref, bf16[2,384,2048]{2,1,0:T(8,128)(2,1)} %down_ref.3, bf16[16,80,2048]{2,1,0:T(8,128)(2,1)} %all_to_all.20.arr_ref), custom_call_target="tpu_custom_call" | custom-call | tf_op jit(solution)/shard_map/backward/pallas_call | solution.py:367
  172.3 0.0 reduce-scatter.2.cloned.1.call-update
  172.4 0.1 copy.12
  172.5 0.0 all-gather.2.cloned.1.call-done
  172.5 1.7 copy.14
  174.2 1.3 fusion.1
  175.6 60.1 %reduce-scatter.2.cloned.1.call-done = bf16[256,768]{1,0:T(8,128)(2,1)} async-done(((bf16[4096,768]{1,0:T(8,128)(2,1)}), bf16[256,768]{1,0:T(8,128)(2,1)}) %reduce-scatter.2.cloned.1.call-update) | async-done | bytes 393232 | tf_op jit(solution)/shard_map/reduce_scatter | solution.py:383
  235.6 1.9 slice_convert_fusion
  (6 shorter events, 0.1 us)
Async XLA Ops:
  7.2 165.3 %all-gather.2.cloned.1.call-start = ((), (), s32[]{:S(2)}) async-start(), calls=%async_computation.6 | async-start | bytes 1671168 | tf_op jit(solution)/shard_map/all_gather | solution.py:324
  7.2 1.1 copy-start
  8.3 0.7 copy-start.1
  9.0 0.7 copy-start.2
  9.7 0.7 copy-start.3
  84.9 27.7 %copy-start.4 = (s32[3]{0:T(128)S(1)}, s32[3]{0:T(128)}, u32[]{:S(2)}) copy-start(s32[3]{0:T(128)} %len_ref.3) | copy-start | bytes 40
  98.6 14.0 %all-to-all-start.1 = ((f32[16,4,2048]{2,1,0:T(4,128)}), f32[16,4,2048]{2,1,0:T(4,128)S(1)}, u32[]{:S(2)}, u32[]{:S(2)}) async-start(f32[16,4,2048]{2,1,0:T(4,128)} %get-tuple-element.14), calls=%async_computation.1 | async-start | bytes 1048576 | tf_op jit(solution)/shard_map/all_to_all | solution.py:325
  114.0 26.8 %all-to-all-start.2 = ((f32[16,4,2048]{2,1,0:T(4,128)}), f32[16,4,2048]{2,1,0:T(4,128)S(1)}, u32[]{:S(2)}, u32[]{:S(2)}) async-start(f32[16,4,2048]{2,1,0:T(4,128)} %pool.1), calls=%async_computation.2 | async-start | bytes 1048576 | tf_op jit(solution)/shard_map/all_to_all | solution.py:336
  122.6 113.0 %reduce-scatter.2.cloned.1.call-start = ((), (), s32[]{:S(2)}) async-start(), calls=%async_computation.5 | async-start | bytes 6684672 | tf_op jit(solution)/shard_map/reduce_scatter | solution.py:383
Sparse Core Ops, SparseCore 0:
  98.7 44.9 all-gather.1
  172.5 63.1 reduce-scatter.1

commit v2 on v1

v2 whole, which is shorter than its diff:
```python
import functools

import jax
import jax.numpy as jnp
from jax import lax
from jax.experimental import pallas as pl
from jax.experimental.pallas import tpu as pltpu
from jax.sharding import Mesh
from jax.sharding import PartitionSpec as P

inv_temp = 20.0
loss_scale = 128.0
norm_eps = 1e-06

BF = jnp.bfloat16
F32 = jnp.float32
I32 = jnp.int32

PART = 80
WIN = 48
SHIFT = 32
META = 44
SEQS = 3
EXPERTS = 32
LINE = 4
NOTE = 16

NN = (((1,), (0,)), ((), ()))
NT = (((1,), (1,)), ((), ()))
TN = (((0,), (0,)), ((), ()))


def iota(shape, axis):
    return lax.broadcasted_iota(I32, shape, axis)


def mm(a, b, dims=NN):
    return lax.dot_general(a, b, dims, preferred_element_type=F32)


def split2(value):
    high = value.astype(BF)
    return high, (value - high.astype(F32)).astype(BF)


def split3(value):
    high = value.astype(BF)
    rest = value - high.astype(F32)
    mid = rest.astype(BF)
    return high, mid, (rest - mid.astype(F32)).astype(BF)


def third(row):
    return (row * 43) >> 7


def window_row(expert, place):
    odd = (expert & 1) == 1
    return jnp.where(odd, jnp.where(place < 32, place + 16, place - 26), place)


def prepare_kernel(length, len_ref, ids_ref, rw_ref, hid_ref, out_ref, sum_ref):
    top, tok = ids_ref.shape
    experts = EXPERTS
    pos = iota((1, tok), 1)
    seq = jnp.zeros((1, tok), I32)
    bound = jnp.full((1, tok), len_ref[0], I32)
    for s in range(1, len_ref.shape[0]):
        later = pos >= s * length
        seq = seq + later.astype(I32)
        bound = jnp.where(later, len_ref[s], bound)
    valid = pos - seq * length < bound
    ids = jnp.where(valid, ids_ref[...], -1)
    names = iota((experts, tok), 0)
    hits = [(ids[k : k + 1] == names).astype(F32) for k in range(top)]
    count = functools.reduce(jnp.add, hits)
    earlier = (iota((tok, tok), 0) < iota((tok, tok), 1)).astype(BF)
    before = mm(count.astype(BF), earlier)
    weight = rw_ref[...].astype(F32)
    lane = iota((128, tok), 0)
    marks = (seq + 1).astype(F32)
    meta = jnp.zeros((2 * experts, 128), F32)
    spots = []
    for k in range(top):
        place = jnp.sum(hits[k] * before, axis=0, keepdims=True).astype(I32)
        for m in range(k):
            place = place + (ids[m : m + 1] == ids[k : k + 1]).astype(I32)
        spot = window_row(ids[k : k + 1], place)
        spots.append(spot)
        chosen = (lane == spot).astype(BF)
        both = jnp.concatenate([hits[k] * weight[k : k + 1], hits[k] * marks], axis=0)
        meta = meta + mm(both.astype(BF), chosen, NT)
    meta = meta.astype(BF)
    member = jnp.logical_and(iota((8, tok), 0) == seq, valid).astype(BF)
    sum_ref[...] = mm(member, hid_ref[...])
    note = jnp.concatenate([ids.astype(F32), jnp.concatenate(spots, axis=0).astype(F32)], axis=0).astype(BF)
    out_ref[:tok, :] = hid_ref[...]
    out_ref[tok:, :] = jnp.zeros((NOTE, hid_ref.shape[1]), BF)
    out_ref[tok:, 0:tok] = note
    for c in range(2 * experts // NOTE):
        out_ref[tok:, 256 + c * 128 : 384 + c * 128] = meta[c * NOTE : (c + 1) * NOTE]


def select_kernel(at_ref, *refs):
    inputs, outputs = refs[:LINE], refs[LINE:]
    tok = inputs[0].shape[0] - NOTE
    x, y, core = at_ref[0], at_ref[1], at_ref[2]
    m = pl.program_id(0)
    for source in range(LINE):
        message = inputs[source]

        @pl.when(m == source)
        def _(message=message):
            note = message[tok:, 0:tok].astype(F32)
            ids = note[0 : NOTE // 2].astype(I32)
            spots = note[NOTE // 2 :].astype(I32)
            device = ids >> 1
            row = (ids & 1) * SHIFT + spots
            line = iota((PART, tok), 0)
            meta = jnp.concatenate(
                [message[tok:, 256 + c * 128 : 384 + c * 128] for c in range(2 * EXPERTS // NOTE)], axis=0
            )
            rows = iota((PART, 2 * EXPERTS), 0)
            col = iota((PART, 2 * EXPERTS), 1)
            mark = (col >= EXPERTS).astype(I32)
            expert = col - EXPERTS * mark
            noted = rows == META + 2 * (expert & 1) + mark
            wanted = []
            chosen = []
            for k in range(LINE):
                j = jnp.where(
                    core == 0,
                    x * LINE + ((y + k) & (LINE - 1)),
                    ((x + k) & (LINE - 1)) * LINE + y,
                )
                spot = jnp.where(device == j, row, -1)
                picked = line == spot[0:1]
                for t in range(1, NOTE // 2):
                    picked = jnp.logical_or(picked, line == spot[t : t + 1])
                wanted.append(picked.astype(BF))
                chosen.append(jnp.logical_and(noted, expert >> 1 == j).astype(BF))
            out = mm(jnp.concatenate(wanted, axis=0), message[:tok, :])
            extra = mm(jnp.concatenate(chosen, axis=0), meta)
            for k in range(LINE):
                part = slice(k * PART, (k + 1) * PART)
                outputs[k][0, :, 128:] = out[part, 128:].astype(BF)
                outputs[k][0, :, :128] = (out[part, :128] + extra[part]).astype(BF)


def forward_kernel(groups, at_ref, *refs):
    arrived = refs[:LINE]
    gate_ref, up_ref, down_ref, part_ref, a_ref, keep_ref, w_ref, x_ref, acc_ref = refs[LINE:]
    e = pl.program_id(0)
    here_x, here_y, core = at_ref[0], at_ref[1], at_ref[2]
    rows = groups * WIN
    owned = groups * SEQS
    chunks = x_ref.shape[2] // 128

    def run(h):
        window = slice(h * SHIFT, h * SHIFT + WIN)
        for r in range(groups):
            x_ref[0, r * WIN : (r + 1) * WIN, :] = arrived[r % LINE][r // LINE, window, :]
        x = x_ref[0]
        gate = mm(x, gate_ref[0])
        up = mm(x, up_ref[0])
        sigma = jax.nn.sigmoid(gate)
        act = gate * sigma
        slope = sigma * (1.0 + gate * (1.0 - sigma))
        ff = gate.shape[1]
        keep_ref[0, :, 0:ff] = (up * slope).astype(BF)
        keep_ref[0, :, ff : 2 * ff] = act.astype(BF)
        inner = (act * up).astype(BF)
        at = META - 32 + 2 * h
        tails = [arrived[r % LINE][r // LINE, 32:48, 0:128].astype(F32) for r in range(groups)]
        wrow = jnp.concatenate([t[at : at + 1] for t in tails], axis=0).astype(BF)
        srow = jnp.concatenate([t[at + 1 : at + 2] for t in tails], axis=0).astype(BF)

        def relative(shape):
            block = third(iota(shape, 0))
            by_x = (here_x - (block >> 2)) & 3
            by_y = (here_y - (block & 3)) & 3
            return jnp.where(core == 0, by_x * LINE + by_y, by_y * LINE + by_x)

        owner = (relative((owned, groups)) == iota((owned, groups), 1)).astype(BF)
        wrep = mm(owner, wrow)
        srep = mm(owner, srow)
        row = iota((owned, 128), 0)
        number = (row - SEQS * third(row) + 1).astype(F32)
        picked = jnp.where(srep == number, wrep, 0.0).astype(BF)
        spread = jnp.zeros((128, rows), jnp.bool_)
        line, col = iota((128, rows), 0), iota((128, rows), 1)
        for g in range(groups):
            spread = jnp.logical_or(spread, col == line + g * WIN)
        spread = jnp.logical_and(spread, line < WIN).astype(BF)
        start = relative((owned, rows)) * WIN
        col = iota((owned, rows), 1)
        inside = jnp.logical_and(col >= start, col < start + WIN)
        weights = jnp.where(inside, mm(picked, spread), 0.0).astype(BF)
        w_ref[0] = weights
        a = mm(weights, inner)
        high, low = split2(a)
        a_ref[...] = high
        both = mm(jnp.concatenate([high, low], axis=0), down_ref[0])
        total = both[:owned] + both[owned:]
        if h == 0:
            acc_ref[...] = total
        else:
            total = total + acc_ref[...]
            for g in range(groups):
                for c in range(chunks):
                    part_ref[g, c * SEQS : (c + 1) * SEQS, :] = total[
                        g * SEQS : (g + 1) * SEQS, c * 128 : (c + 1) * 128
                    ]

    @pl.when(e == 0)
    def _():
        run(0)

    @pl.when(e == 1)
    def _():
        run(1)


def pool_kernel(len_ref, pos_ref, recv_ref, sum_ref, out_ref, note_ref):
    groups, packed, _ = recv_ref.shape
    chunks = packed // SEQS
    total = recv_ref[0]
    for g in range(1, groups):
        total = total + recv_ref[g]
    note_ref[0:packed, :] = total
    total = jnp.concatenate([note_ref[c * SEQS : (c + 1) * SEQS, :] for c in range(chunks)], axis=1)
    row = iota((SEQS, 1), 0)
    inverse = jnp.zeros((SEQS, 1), F32)
    for s in range(SEQS):
        inverse = jnp.where(row == s, 1.0 / jnp.full((SEQS, 1), len_ref[s], I32).astype(F32), inverse)
    pooled = (total + sum_ref[0:SEQS, :]) * inverse
    scale = lax.rsqrt(jnp.sum(pooled * pooled, axis=1, keepdims=True) + norm_eps)
    positive = pos_ref[0]
    col = iota((1, 128), 1)
    note = jnp.where(col == 0, (positive >> 1) * SEQS + 1 + (positive & 1), 0)
    for s in range(SEQS):
        note = jnp.where(col == 1 + s, len_ref[s], note)
    note = note.astype(F32)
    for place, piece in enumerate(split3(scale)):
        piece = piece.astype(F32)
        for s in range(SEQS):
            note = jnp.where(col == 4 * (place + 1) + 1 + s, piece[s : s + 1], note)
    embed = pooled * scale
    for c in range(chunks):
        note_ref[c * SEQS : (c + 1) * SEQS, :] = embed[:, c * 128 : (c + 1) * 128]
    note_ref[packed:, :] = jnp.where(iota((NOTE, 128), 0) == 0, note, 0.0)
    value = note_ref[...].astype(BF)
    for g in range(groups):
        out_ref[g] = value


def contrast_kernel(at_ref, recv_ref, loss_ref, out_ref, all_ref, grad_ref, note_ref):
    groups = recv_ref.shape[0]
    packed = recv_ref.shape[1] - NOTE
    chunks = packed // SEQS
    owned = groups * SEQS
    me = at_ref[0]
    notes = []
    for g in range(groups):
        value = recv_ref[g].astype(F32)
        notes.append(value[packed : packed + 1])
        for c in range(chunks):
            all_ref[g * SEQS : (g + 1) * SEQS, c * 128 : (c + 1) * 128] = value[c * SEQS : (c + 1) * SEQS]
    notes = jnp.concatenate(notes, axis=0).astype(BF)

    def sort(shape, axis):
        place = iota(shape, axis)
        return place - SEQS * third(place)

    owner = (third(iota((owned, groups), 0)) == iota((owned, groups), 1)).astype(BF)
    notes = mm(owner, notes)
    lane = iota((owned, 128), 1)
    sub = sort((owned, 128), 0)
    target = jnp.sum(jnp.where(lane == 0, notes, 0.0), axis=1, keepdims=True)
    length = jnp.sum(jnp.where(lane == 1 + sub, notes, 0.0), axis=1, keepdims=True)
    pieces = jnp.logical_and(lane > 4, lane < 16)
    scale = jnp.sum(jnp.where(jnp.logical_and(pieces, (lane & 3) == 1 + sub), notes, 0.0), axis=1, keepdims=True)
    wide = all_ref[...]
    embed = wide.astype(BF)
    scores = mm(embed, embed, NT) * inv_temp
    passage = sort((owned, owned), 1) > 0
    total = jnp.log(jnp.sum(jnp.where(passage, jnp.exp(scores), 0.0), axis=1, keepdims=True))
    hit = (iota((owned, owned), 1).astype(F32) == target).astype(F32)
    losses = total - jnp.sum(hit * scores, axis=1, keepdims=True)
    wanted = iota((owned, 128), 0) == me * SEQS
    loss_ref[...] = jnp.sum(jnp.where(wanted, losses, 0.0), axis=0, keepdims=True)
    coeff = (jnp.where(passage, jnp.exp(scores - total), 0.0) - hit) * (loss_scale * inv_temp)
    coeff = jnp.where(sort((owned, owned), 0) == 0, coeff, 0.0)
    coeff = coeff + coeff.T
    three = mm(jnp.concatenate(split3(coeff), axis=0), embed)
    grad = three[:owned] + three[owned : 2 * owned] + three[2 * owned :]
    along = jnp.sum(wide * grad, axis=1, keepdims=True)
    grad = (grad - wide * along) * (scale / length)
    all_ref[...] = grad
    for g in range(groups):
        grad_ref[g] = grad[g * SEQS : (g + 1) * SEQS]
    own = grad_ref[me]
    for c in range(chunks):
        note_ref[c * SEQS : (c + 1) * SEQS, :] = own[:, c * 128 : (c + 1) * 128]
    note_ref[packed:, :] = all_ref[:, pl.ds(pl.multiple_of(me * 128, 128), 128)]
    value = note_ref[...].astype(BF)
    for g in range(out_ref.shape[0]):
        out_ref[g] = value


def weight_parts(core, x_ref, pre_ref, mine_ref, other_ref):
    for e in range(pre_ref.shape[0]):
        part = mm(x_ref[e], pre_ref[e], TN)
        half = part.shape[0] // 2
        first, second = part[:half], part[half:]
        mine_ref[0, e] = jnp.where(core == 0, first, second).astype(BF)
        other_ref[0, e] = jnp.where(core == 0, second, first).astype(BF)


def first_kernel(at_ref, recv_ref, keep_ref, w_ref, down_ref, x_ref, pre_ref, mine_ref, other_ref, grad_ref):
    ff = down_ref.shape[1]
    chunks = grad_ref.shape[1] // 128
    for g in range(recv_ref.shape[0]):
        value = recv_ref[g].astype(F32)
        for c in range(chunks):
            grad_ref[g * SEQS : (g + 1) * SEQS, c * 128 : (c + 1) * 128] = value[c * SEQS : (c + 1) * SEQS]
    grad = grad_ref[...].astype(BF)
    for e in range(keep_ref.shape[0]):
        back = mm(grad, down_ref[e], NT)
        high, low = split2(back)
        two = jnp.concatenate([high, low], axis=0)
        weights = w_ref[e]
        inner = mm(jnp.concatenate([weights, weights], axis=0), two, TN)
        pre_ref[e, :, 0:ff] = (inner * keep_ref[e, :, 0:ff].astype(F32)).astype(BF)
        pre_ref[e, :, ff : 2 * ff] = (inner * keep_ref[e, :, ff : 2 * ff].astype(F32)).astype(BF)
    weight_parts(at_ref[2], x_ref, pre_ref, mine_ref, other_ref)


def more_kernel(at_ref, pre_ref, x_ref, mine_ref, other_ref):
    weight_parts(at_ref[2], x_ref, pre_ref, mine_ref, other_ref)


def body(hidden, w_gate, w_up, w_down, expert_ids, route_weight, seq_len, positive):
    dp, ep = ("z", "core"), ("x", "y")
    tok, width = hidden.shape
    local, _, ff = w_gate.shape
    groups = lax.axis_size(ep)
    members = lax.axis_size(dp)
    top = expert_ids.shape[1]
    length = tok // SEQS
    owned = groups * SEQS
    packed = SEQS * width // 128
    rows = groups * WIN
    me = lax.axis_index(dp).astype(I32).reshape(1)
    smem = pl.BlockSpec(memory_space=pltpu.SMEM)
    big = pltpu.CompilerParams(vmem_limit_bytes=50 * 1024 * 1024)

    at = jnp.stack([lax.axis_index(a) for a in ("x", "y", "core", "z")]).astype(I32)
    vmem = pl.BlockSpec(memory_space=pltpu.VMEM)
    message, hidden_sum = pl.pallas_call(
        functools.partial(prepare_kernel, length),
        out_shape=(
            jax.ShapeDtypeStruct((tok + NOTE, width), BF),
            jax.ShapeDtypeStruct((8, width), F32),
        ),
        in_specs=[smem, vmem, vmem, vmem],
        out_specs=(vmem, vmem),
        name="prepare",
    )(seq_len, expert_ids.T, route_weight.T, hidden)

    def ahead(value, k, turned):
        pairs = []
        for core in range(2):
            for x in range(LINE):
                for y in range(LINE):
                    to = ((x + k) % LINE, y) if core == turned else (x, (y + k) % LINE)
                    pairs.append(((core * LINE + x) * LINE + y, (core * LINE + to[0]) * LINE + to[1]))
        return lax.ppermute(value, ("core", "x", "y"), pairs)

    gathered = {0: message}
    for k in (1, 3, 2):
        gathered[k] = ahead(message, k, 0)
    picked = pl.pallas_call(
        select_kernel,
        grid=(LINE,),
        out_shape=[jax.ShapeDtypeStruct((LINE, PART, width), BF)] * LINE,
        in_specs=[smem] + [pl.BlockSpec((tok + NOTE, width), lambda m: (0, 0))] * LINE,
        out_specs=[pl.BlockSpec((1, PART, width), lambda m: (m, 0, 0))] * LINE,
        compiler_params=big,
        name="select",
    )(at, *[gathered[k] for k in range(LINE)])
    arrived = {0: picked[0]}
    for k in (1, 3, 2):
        arrived[k] = ahead(picked[k], k, 1)

    partial, summed, keep, weights, rows_in = pl.pallas_call(
        functools.partial(forward_kernel, groups),
        grid=(local,),
        out_shape=(
            jax.ShapeDtypeStruct((groups, packed, 128), F32),
            jax.ShapeDtypeStruct((owned, local * ff), BF),
            jax.ShapeDtypeStruct((local, rows, 2 * ff), BF),
            jax.ShapeDtypeStruct((local, owned, rows), BF),
            jax.ShapeDtypeStruct((local, rows, width), BF),
        ),
        in_specs=[smem]
        + [pl.BlockSpec((LINE, PART, width), lambda e: (0, 0, 0))] * LINE
        + [
            pl.BlockSpec((1, width, ff), lambda e: (e, 0, 0)),
            pl.BlockSpec((1, width, ff), lambda e: (e, 0, 0)),
            pl.BlockSpec((1, ff, width), lambda e: (e, 0, 0)),
        ],
        out_specs=(
            pl.BlockSpec((groups, packed, 128), lambda e: (0, 0, 0)),
            pl.BlockSpec((owned, ff), lambda e: (0, e)),
            pl.BlockSpec((1, rows, 2 * ff), lambda e: (e, 0, 0)),
            pl.BlockSpec((1, owned, rows), lambda e: (e, 0, 0)),
            pl.BlockSpec((1, rows, width), lambda e: (e, 0, 0)),
        ),
        scratch_shapes=[pltpu.VMEM((owned, width), F32)],
        compiler_params=big,
        name="forward",
    )(at, *[arrived[k] for k in range(LINE)], w_gate, w_up, w_down)

    all_summed = lax.all_gather(summed, dp, axis=0, tiled=True)
    returned = lax.all_to_all(partial, ep, split_axis=0, concat_axis=0, tiled=True)

    pooled = pl.pallas_call(
        pool_kernel,
        out_shape=jax.ShapeDtypeStruct((members, packed + NOTE, 128), BF),
        in_specs=[smem, smem, vmem, vmem],
        out_specs=vmem,
        scratch_shapes=[pltpu.VMEM((packed + NOTE, 128), F32)],
        compiler_params=big,
        name="pool",
    )(seq_len, positive, returned, hidden_sum)
    column = lax.all_to_all(pooled, dp, split_axis=0, concat_axis=0, tiled=True)

    noted = packed + members * SEQS
    loss, note = pl.pallas_call(
        contrast_kernel,
        out_shape=(
            jax.ShapeDtypeStruct((1, 128), F32),
            jax.ShapeDtypeStruct((groups, noted, 128), BF),
        ),
        in_specs=[smem, vmem],
        out_specs=(vmem, vmem),
        scratch_shapes=[
            pltpu.VMEM((members * SEQS, width), F32),
            pltpu.VMEM((members, SEQS, width), F32),
            pltpu.VMEM((noted, 128), F32),
        ],
        compiler_params=big,
        name="contrast",
    )(me, column)
    spread = lax.all_to_all(note, ep, split_axis=0, concat_axis=0, tiled=True)
    columns = spread[:, packed:].reshape(groups, members, SEQS, 128)
    columns = jnp.transpose(columns, (1, 0, 2, 3)).reshape(members * owned, 128)

    ring = lax.axis_size("z")
    cols = width // ring
    piece = (local, cols // 2, 2 * ff)

    def shard_spec(order):
        return pl.BlockSpec((local, rows, cols), lambda i, at: (0, 0, (at[3] + order(i)) & (ring - 1)))

    def parts_spec():
        return pl.BlockSpec((1,) + piece, lambda i, at: (i, 0, 0, 0))

    def cost(shards, extra=0):
        flops = shards * local * 2 * rows * cols * 2 * ff
        return pl.CostEstimate(flops=flops, bytes_accessed=shards * 4 * local * rows * cols + extra, transcendentals=0)

    pre, mine, other = pl.pallas_call(
        first_kernel,
        grid_spec=pltpu.PrefetchScalarGridSpec(
            num_scalar_prefetch=1,
            grid=(1,),
            in_specs=[
                pl.BlockSpec((groups, noted, 128), lambda i, at: (0, 0, 0)),
                pl.BlockSpec((local, rows, 2 * ff), lambda i, at: (0, 0, 0)),
                pl.BlockSpec((local, owned, rows), lambda i, at: (0, 0, 0)),
                pl.BlockSpec((local, ff, width), lambda i, at: (0, 0, 0)),
                shard_spec(lambda i: 4),
            ],
            out_specs=[
                pl.BlockSpec((local, rows, 2 * ff), lambda i, at: (0, 0, 0)),
                parts_spec(),
                parts_spec(),
            ],
            scratch_shapes=[pltpu.VMEM((owned, width), F32)],
        ),
        out_shape=(
            jax.ShapeDtypeStruct((local, rows, 2 * ff), BF),
            jax.ShapeDtypeStruct((1,) + piece, BF),
            jax.ShapeDtypeStruct((1,) + piece, BF),
        ),
        cost_estimate=cost(1, 16 * 1024 * 1024),
        compiler_params=big,
        name="first_parts",
    )(at, spread, keep, weights, w_down, rows_in)

    def more(shards, order, name):
        return pl.pallas_call(
            more_kernel,
            grid_spec=pltpu.PrefetchScalarGridSpec(
                num_scalar_prefetch=1,
                grid=(shards,),
                in_specs=[
                    pl.BlockSpec((local, rows, 2 * ff), lambda i, at: (0, 0, 0)),
                    shard_spec(order),
                ],
                out_specs=[parts_spec(), parts_spec()],
            ),
            out_shape=[jax.ShapeDtypeStruct((shards,) + piece, BF)] * 2,
            cost_estimate=cost(shards),
            compiler_params=big,
            name=name,
        )(at, pre, rows_in)

    def swap(value):
        return lax.ppermute(value, "core", [(0, 1), (1, 0)])

    def along(value, k):
        return lax.ppermute(value, "z", [(i, (i + k) % ring) for i in range(ring)])

    def total(*values):
        return sum(v.astype(F32) for v in values)

    theirs = swap(other)
    held, sent = more(2, lambda i: 3 + 2 * i, "parts_three")
    up, down = total(mine[0, 0], theirs[0, 0]).astype(BF), total(mine[0, 1], theirs[0, 1]).astype(BF)
    up, down, pre, sent = lax.optimization_barrier((up, down, pre, sent))
    up, down, got = along(up, 1), along(down, -1), swap(sent)
    later = more(2, lambda i: 2 + 4 * i, "parts_two")
    up = jnp.stack([total(held[0, 0], got[0, 0], up), total(held[0, 1], got[0, 1])]).astype(BF)
    down = jnp.stack([total(held[1, 0], got[1, 0]), total(held[1, 1], got[1, 1], down)]).astype(BF)
    up, down, pre, later = lax.optimization_barrier((up, down, pre, later))
    held, sent = later
    up, down, got = along(up, 1), along(down, -1), swap(sent)
    later = more(3, lambda i: jnp.where(i == 0, 1, 7 * (2 - i)), "parts_one")
    up = total(held[0], got[0], up).astype(BF)
    down = total(held[1], got[1], down).astype(BF)
    up, down, later = lax.optimization_barrier((up, down, later))
    held, sent = later
    up, down, got = along(up, 1), along(down, -1), swap(sent)
    up = total(held[0], got[0], up).astype(BF)
    down = total(held[1], got[1], down).astype(BF)
    up, down = lax.optimization_barrier((up, down))
    up, down = along(up, 1), along(down, -1)
    reduced = total(held[2], got[2], up, down)
    grad_down = jnp.einsum(
        "qef,qd->efd",
        all_summed.reshape(members * owned, local, ff),
        columns,
        preferred_element_type=F32,
    )
    return (
        loss[0, :1],
        reduced[:, :, :ff],
        reduced[:, :, ff:],
        grad_down,
    )


def solution(mesh):
    mesh = Mesh(mesh.devices.reshape(8, 2, 4, 4), ("z", "core", "x", "y"))
    dp, ep = ("z", "core"), ("x", "y")
    tokens = P(dp + ep)
    placed = (
        P(dp + ep, None),
        P(ep, None, None),
        P(ep, None, None),
        P(ep, None, None),
        P(dp + ep, None),
        P(dp + ep, None),
        tokens,
        tokens,
    )
    return jax.shard_map(
        body,
        mesh=mesh,
        in_specs=placed,
        out_specs=(tokens, P(ep, dp, None), P(ep, dp, None), P(ep, None, dp)),
        check_vma=False,
    )
```

time: 245 us -> 211 us (0.86)
  blocking collectives: 84.3 us -> 14.3 us
  starting transfers between devices: 14.7 us -> 40.2 us
  Pallas kernels: 36.6 us -> 43.4 us
  other arithmetic: 1.97 us -> 5.14 us
    all_to_all x2 -> x1, blocking collectives: 84.3 us -> 14.3 us  [body(): spread = lax.all_to_all(note, ep, split_axis=0, concat_axis=0, tiled=True)]
    ppermute x0 -> x18, waiting for transfers between devices: none -> 62.6 us  [the longest x6 43.4 us: ahead(): return lax.ppermute(value, ('core', 'x', 'y'), pairs)]
    reduce_scatter x1 -> x0, waiting for transfers between devices: 60.1 us -> none  [body(): lax.psum_scatter(partials.reshape(shards * local * 128, 2 * ff), dp, scat...]
    ppermute x0 -> x18, starting transfers between devices: none -> 24.9 us  [the longest x8 13.6 us: along(): return lax.ppermute(value, 'z', [(i, (i + k) % ring) for i in range(ring)])]
    all_to_all x1, waiting for transfers between devices: 18.1 us -> 11.1 us  [body(): column = lax.all_to_all(pooled, dp, split_axis=0, concat_axis=0, tiled=True)]
    pallas_call x4 -> x8, Pallas kernels: 35.4 us -> 41.9 us  [the longest x1 14.3 us: body(): pl.pallas_call(functools.partial(forward_kernel, groups), grid=(local,),...]
    all_gather x1, waiting for transfers between devices: 0.02 us -> 2.98 us  [body(): all_summed = lax.all_gather(summed, dp, axis=0, tiled=True)]
  transfers between devices with their start and end apart: 4 -> 21, of which waited for: 3 -> 13; matrix products, arithmetic and copies ran while one was open for 1% -> 4% of each run, Pallas kernels for 7% -> 6%
where the time goes in v2:
time: 211 us; the launch traced here: 209 us
  waiting for transfers between devices  83.1 us (39%)
  Pallas kernels  43.4 us (21%)
  starting transfers between devices  40.2 us (19%)
  between operations  14.8 us (7%)
  blocking collectives  14.3 us (7%)
  local copies, waits for them, and re-layouts  6.07 us (3%)
  other arithmetic  5.14 us (2%)
  matrix products  2.15 us (1%)
    ppermute x6, waiting for transfers between devices, ahead(): return lax.ppermute(value, ('core', 'x', 'y'), pairs)  43.4 us
    ppermute x8, waiting for transfers between devices, along(): return lax.ppermute(value, 'z', [(i, (i + k) % ring) for i in range(ring)])  19.2 us
    all_to_all x1, blocking collectives, body(): spread = lax.all_to_all(note, ep, split_axis=0, concat_axis=0, tiled=True)  14.3 us
    pallas_call x1, Pallas kernels, body(): pl.pallas_call(functools.partial(forward_kernel, groups), grid=(local,),...  14.3 us
    ppermute x8, starting transfers between devices, along(): return lax.ppermute(value, 'z', [(i, (i + k) % ring) for i in range(ring)])  13.6 us
    pallas_call x3, Pallas kernels, more(): pl.pallas_call(more_kernel, grid_spec=pltpu.PrefetchScalarGridSpec(num_sc...  12.8 us
    all_to_all x1, waiting for transfers between devices, body(): column = lax.all_to_all(pooled, dp, split_axis=0, concat_axis=0, tiled=True)  11.1 us
    ppermute x6, starting transfers between devices, ahead(): return lax.ppermute(value, ('core', 'x', 'y'), pairs)  10.7 us
  transfers between devices with their start and end apart: 21, of which 13 were waited for; matrix products, arithmetic and copies ran while one was open for 4% of the time, Pallas kernels for 6%

profile of v2, /device:TPU:4, one launch (start us, length us, event | category | flops | bytes accessed | tf_op | source)
XLA Modules:
  0.0 209.3 jit_solution(18407863195198175999)
XLA Ops:
  7.2 2.5 %prepare.1 = (bf16[160,2048]{1,0:T(8,128)(2,1)}, f32[8,2048]{1,0:T(8,128)}) custom-call(s32[3]{0:T(128)} %len_ref.3, s32[8,144]{1,0:T(8,128)} %bitcast.61, bf16[8,144]{1,0:T(8,128)(2,1)} %bitcast.62, bf16[144,2048]{1,0:T(8,128)(2,1)} %hid_ref.1), custom_call_target="tpu_custom_call" | custom-call | tf_op jit(solution)/shard_map/prepare/pallas_call | solution.py:360
  10.2 2.7 %collective-permute-start.1 = (bf16[160,2048]{1,0:T(8,128)(2,1)}, bf16[160,2048]{1,0:T(8,128)(2,1)S(1)}, u32[]{:S(2)}, u32[]{:S(2)}) collective-permute-start(bf16[160,2048]{1,0:T(8,128)(2,1)} %get-tuple-element.41.refs_0_), channel_id=1, source_target_pairs={{0,8},{1,9},{2,10},{3,11},{4,12},{5,13},{6,14},{7,15},{8,0},{9,1},... | collective-permute-start | bytes 1966088 | tf_op jit(solution)/shard_map/ppermute | solution.py:378
  13.0 1.6 collective-permute-start
  14.7 5.8 %collective-permute-done.2.refs_3_ = bf16[160,2048]{1,0:T(8,128)(2,1)S(1)} collective-permute-done((bf16[160,2048]{1,0:T(8,128)(2,1)}, bf16[160,2048]{1,0:T(8,128)(2,1)S(1)}, u32[]{:S(2)}, u32[]{:S(2)}) %collective-permute-start.2) | collective-permute-done | bytes 655392 | tf_op jit(solution)/shard_map/ppermute | solution.py:378
  20.5 2.1 %collective-permute-done.1.refs_2_ = bf16[160,2048]{1,0:T(8,128)(2,1)S(1)} collective-permute-done((bf16[160,2048]{1,0:T(8,128)(2,1)}, bf16[160,2048]{1,0:T(8,128)(2,1)S(1)}, u32[]{:S(2)}, u32[]{:S(2)}) %collective-permute-start.1) | collective-permute-done | bytes 655392 | tf_op jit(solution)/shard_map/ppermute | solution.py:378
  22.6 6.9 %collective-permute-done.refs_1_ = bf16[160,2048]{1,0:T(8,128)(2,1)S(1)} collective-permute-done((bf16[160,2048]{1,0:T(8,128)(2,1)}, bf16[160,2048]{1,0:T(8,128)(2,1)S(1)}, u32[]{:S(2)}, u32[]{:S(2)}) %collective-permute-start) | collective-permute-done | bytes 655392 | tf_op jit(solution)/shard_map/ppermute | solution.py:378
  30.6 4.8 %select.1 = (bf16[4,80,2048]{2,1,0:T(8,128)(2,1)S(1)}, bf16[4,80,2048]{2,1,0:T(8,128)(2,1)}, bf16[4,80,2048]{2,1,0:T(8,128)(2,1)}, bf16[4,80,2048]{2,1,0:T(8,128)(2,1)}) custom-call(s32[4]{0:T(128)S(1)} %pad_add_fusion.at_ref, bf16[160,2048]{1,0:T(8,128)(2,1)S(1)} %copy-done.1, bf16[160,2048]{1,0:T(8,128)(2,1)S(1)} %collective-permute-done.refs_1_, ...), custom_call_target="tpu_custom_call" | custom-call | tf_op jit(solution)/shard_map/select/pallas_call | solution.py:383
  35.5 1.6 collective-permute-start.3
  37.1 2.9 %collective-permute-start.4 = (bf16[4,80,2048]{2,1,0:T(8,128)(2,1)}, bf16[4,80,2048]{2,1,0:T(8,128)(2,1)S(1)}, u32[]{:S(2)}, u32[]{:S(2)}) collective-permute-start(bf16[4,80,2048]{2,1,0:T(8,128)(2,1)} %get-tuple-element.44), channel_id=1, source_target_pairs={{0,2},{1,3},{2,0},{3,1},{4,6},{5,7},{6,4},{7,5},{8,10},{9,11},{10,... | collective-permute-start | bytes 3932168 | tf_op jit(solution)/shard_map/ppermute | solution.py:378
  41.3 13.2 %collective-permute-done.3.refs_1_ = bf16[4,80,2048]{2,1,0:T(8,128)(2,1)S(1)} collective-permute-done((bf16[4,80,2048]{2,1,0:T(8,128)(2,1)}, bf16[4,80,2048]{2,1,0:T(8,128)(2,1)S(1)}, u32[]{:S(2)}, u32[]{:S(2)}) %collective-permute-start.3) | collective-permute-done | bytes 1310752 | tf_op jit(solution)/shard_map/ppermute | solution.py:378
  54.5 15.3 %collective-permute-done.4.refs_2_ = bf16[4,80,2048]{2,1,0:T(8,128)(2,1)S(1)} collective-permute-done((bf16[4,80,2048]{2,1,0:T(8,128)(2,1)}, bf16[4,80,2048]{2,1,0:T(8,128)(2,1)S(1)}, u32[]{:S(2)}, u32[]{:S(2)}) %collective-permute-start.4) | collective-permute-done | bytes 1310752 | tf_op jit(solution)/shard_map/ppermute | solution.py:378
  71.3 14.3 %forward.1 = (f32[16,48,128]{2,1,0:T(8,128)}, bf16[48,768]{1,0:T(8,128)(2,1)}, bf16[2,768,768]{2,1,0:T(8,128)(2,1)}, bf16[2,48,768]{2,1,0:T(8,128)(2,1)S(1)}, bf16[2,768,2048]{2,1,0:T(8,128)(2,1)}) custom-call(s32[4]{0:T(128)S(1)} %pad_add_fusion.at_ref, bf16[4,80,2048]{2,1,0:T(8,128)(2,1)S(1)} %get-tuple-element.42.refs_0_, ...), custom_call_target="tpu_custom_call" | custom-call | tf_op jit(solution)/shard_map/forward/pallas_call | solution.py:396
  85.5 6.7 %all-to-all-start = ((f32[16,48,128]{2,1,0:T(8,128)}), f32[16,48,128]{2,1,0:T(8,128)S(1)}, u32[]{:S(2)}, u32[]{:S(2)}) async-start(f32[16,48,128]{2,1,0:T(8,128)} %get-tuple-element.46), calls=%async_computation | async-start | bytes 786432 | tf_op jit(solution)/shard_map/all_to_all | solution.py:426
  92.9 6.4 %all-to-all-done.recv_ref = f32[16,48,128]{2,1,0:T(8,128)S(1)} async-done(((f32[16,48,128]{2,1,0:T(8,128)}), f32[16,48,128]{2,1,0:T(8,128)S(1)}, u32[]{:S(2)}, u32[]{:S(2)}) %all-to-all-start) | async-done | bytes 393248 | tf_op jit(solution)/shard_map/all_to_all | solution.py:426
  99.3 1.4 pool.1
  100.7 8.6 %all-to-all-start.1 = ((bf16[16,64,128]{2,1,0:T(8,128)(2,1)}), bf16[16,64,128]{2,1,0:T(8,128)(2,1)S(1)}, u32[]{:S(2)}, u32[]{:S(2)}) async-start(bf16[16,64,128]{2,1,0:T(8,128)(2,1)} %pool.1), calls=%async_computation.1 | async-start | bytes 524288 | tf_op jit(solution)/shard_map/all_to_all | solution.py:437
  109.4 11.1 %all-to-all-done.1.recv_ref = bf16[16,64,128]{2,1,0:T(8,128)(2,1)S(1)} async-done(((bf16[16,64,128]{2,1,0:T(8,128)(2,1)}), bf16[16,64,128]{2,1,0:T(8,128)(2,1)S(1)}, u32[]{:S(2)}, u32[]{:S(2)}) %all-to-all-start.1) | async-done | bytes 262176 | tf_op jit(solution)/shard_map/all_to_all | solution.py:437
  120.5 1.5 contrast.1
  121.9 14.3 %all_to_all.15.recv_ref = bf16[16,96,128]{2,1,0:T(8,128)(2,1)S(1)} all-to-all(bf16[16,96,128]{2,1,0:T(8,128)(2,1)S(1)} %get-tuple-element.49), channel_id=1, replica_groups=mesh['z'=8,'core'=2,'x'=4,'y'=4] {'x','y'}, dimensions={0} | all-to-all | bytes 786432 | tf_op jit(solution)/shard_map/all_to_all | solution.py:456
  136.3 6.0 %first_parts.1 = (bf16[2,768,768]{2,1,0:T(8,128)(2,1)S(1)}, bf16[1,2,128,768]{3,2,1,0:T(8,128)(2,1)S(1)}, bf16[1,2,128,768]{3,2,1,0:T(8,128)(2,1)S(1)}) custom-call(s32[4]{0:T(128)S(1)} %pad_add_fusion.at_ref, bf16[16,96,128]{2,1,0:T(8,128)(2,1)S(1)} %all_to_all.15.recv_ref, bf16[2,768,768]{2,1,0:T(8,128)(2,1)} %get-tuple-element.50.keep_ref, ...), custom_call_target="tpu_custom_call" | custom-call | flops 603979776 | bytes 18350080 | tf_op jit(solution)/shard_map/first_parts/pallas_call | solution.py:474
  142.4 3.5 %parts_three.1 = (bf16[2,2,128,768]{3,2,1,0:T(8,128)(2,1)S(1)}, bf16[2,2,128,768]{3,2,1,0:T(8,128)(2,1)S(1)}) custom-call(s32[4]{0:T(128)S(1)} %pad_add_fusion.at_ref, bf16[2,768,768]{2,1,0:T(8,128)(2,1)S(1)} %get-tuple-element.68.pre_ref, bf16[2,768,2048]{2,1,0:T(8,128)(2,1)} %get-tuple-element.52.x_ref), custom_call_target="tpu_custom_call" | custom-call | flops 1207959552 | bytes 3145728 | tf_op jit(solution)/shard_map/parts_three/pallas_call | solution.py:504
  146.5 3.2 %collective-permute-start.9 = (bf16[128,768]{1,0:T(8,128)(2,1)S(1)}, bf16[128,768]{1,0:T(8,128)(2,1)S(1)}, u32[]{:S(2)}, u32[]{:S(2)}) collective-permute-start(bf16[128,768]{1,0:T(8,128)(2,1)S(1)} %get-tuple-element.60), channel_id=1, source_target_pairs={{0,224},{32,0},{64,32},{96,64},{128,96},{160,128},{192,160},{224,1... | collective-permute-start | bytes 589832 | tf_op jit(solution)/shard_map/ppermute | solution.py:525
  149.7 4.1 %parts_two.1 = (bf16[2,2,128,768]{3,2,1,0:T(8,128)(2,1)S(1)}, bf16[2,2,128,768]{3,2,1,0:T(8,128)(2,1)}) custom-call(s32[4]{0:T(128)S(1)} %pad_add_fusion.at_ref, bf16[2,768,768]{2,1,0:T(8,128)(2,1)S(1)} %get-tuple-element.68.pre_ref, bf16[2,768,2048]{2,1,0:T(8,128)(2,1)} %get-tuple-element.52.x_ref), custom_call_target="tpu_custom_call" | custom-call | flops 1207959552 | bytes 3145728 | tf_op jit(solution)/shard_map/parts_two/pallas_call | solution.py:504
  155.8 3.2 %collective-permute-start.12 = (bf16[2,128,768]{2,1,0:T(8,128)(2,1)}, bf16[2,128,768]{2,1,0:T(8,128)(2,1)}, u32[]{:S(2)}, u32[]{:S(2)}) collective-permute-start(bf16[2,128,768]{2,1,0:T(8,128)(2,1)} %get-tuple-element.67), channel_id=1, source_target_pairs={{0,224},{32,0},{64,32},{96,64},{128,96},{160,128},{192,160},{224,1... | collective-permute-start | bytes 1179656 | tf_op jit(solution)/shard_map/ppermute | solution.py:525
  159.0 5.3 %parts_one.1 = (bf16[3,2,128,768]{3,2,1,0:T(8,128)(2,1)S(1)}, bf16[3,2,128,768]{3,2,1,0:T(8,128)(2,1)S(1)}) custom-call(s32[4]{0:T(128)S(1)} %pad_add_fusion.at_ref, bf16[2,768,768]{2,1,0:T(8,128)(2,1)} %copy-done, bf16[2,768,2048]{2,1,0:T(8,128)(2,1)} %get-tuple-element.52.x_ref), custom_call_target="tpu_custom_call" | custom-call | flops 1811939328 | bytes 4718592 | tf_op jit(solution)/shard_map/parts_one/pallas_call | solution.py:504
  164.3 4.4 %collective-permute-done.11 = bf16[2,128,768]{2,1,0:T(8,128)(2,1)S(1)} collective-permute-done((bf16[2,128,768]{2,1,0:T(8,128)(2,1)}, bf16[2,128,768]{2,1,0:T(8,128)(2,1)S(1)}, u32[]{:S(2)}, u32[]{:S(2)}) %collective-permute-start.11) | collective-permute-done | bytes 393248 | tf_op jit(solution)/shard_map/ppermute | solution.py:525
  170.4 3.8 %collective-permute-start.15 = (bf16[2,128,768]{2,1,0:T(8,128)(2,1)S(1)}, bf16[2,128,768]{2,1,0:T(8,128)(2,1)S(1)}, u32[]{:S(2)}, u32[]{:S(2)}) collective-permute-start(bf16[2,128,768]{2,1,0:T(8,128)(2,1)S(1)} %get-tuple-element.74), channel_id=1, source_target_pairs={{0,224},{32,0},{64,32},{96,64},{128,96},{160,128},{192,160},{224,1... | collective-permute-start | bytes 1179656 | tf_op jit(solution)/shard_map/ppermute | solution.py:525
  174.2 12.5 %collective-permute-done.14 = bf16[2,128,768]{2,1,0:T(8,128)(2,1)S(1)} collective-permute-done((bf16[2,128,768]{2,1,0:T(8,128)(2,1)S(1)}, bf16[2,128,768]{2,1,0:T(8,128)(2,1)S(1)}, u32[]{:S(2)}, u32[]{:S(2)}) %collective-permute-start.14) | collective-permute-done | bytes 393248 | tf_op jit(solution)/shard_map/ppermute | solution.py:525
  187.9 3.2 %collective-permute-start.17 = (bf16[2,128,768]{2,1,0:T(8,128)(2,1)}, bf16[2,128,768]{2,1,0:T(8,128)(2,1)}, u32[]{:S(2)}, u32[]{:S(2)}) collective-permute-start(bf16[2,128,768]{2,1,0:T(8,128)(2,1)} %get-tuple-element.76), channel_id=1, source_target_pairs={{0,224},{32,0},{64,32},{96,64},{128,96},{160,128},{192,160},{224,1... | collective-permute-start | bytes 1179656 | tf_op jit(solution)/shard_map/ppermute | solution.py:525
  192.1 3.0 %all-gather.2.cloned.1.call-done = bf16[768,768]{1,0:T(8,128)(2,1)} async-done(((bf16[48,768]{1,0:T(8,128)(2,1)}), bf16[768,768]{1,0:T(8,128)(2,1)}) %all-gather.2.cloned.1.call-update) | async-done | bytes 1179664 | tf_op jit(solution)/shard_map/all_gather | solution.py:425
  195.1 1.6 copy.17
  196.7 2.1 %fusion.14 = f32[2,384,128]{2,1,0:T(8,128)} fusion(bf16[768,2,384]{0,2,1:T(8,128)(2,1)S(1)} %bitcast.59, bf16[768,128,1]{1,0,2:T(8,128)(2,1)} %reshape.107), kind=kOutput, calls=%fused_computation.28 | convolution fusion | flops 150994944 | bytes 1769472 | tf_op jit(solution)/shard_map/qef,qd->efd/dot_general | solution.py:552
  (48 shorter events, 14.6 us)
Async XLA Ops:
  9.7 10.8 %collective-permute-start.2 = (bf16[160,2048]{1,0:T(8,128)(2,1)}, bf16[160,2048]{1,0:T(8,128)(2,1)S(1)}, u32[]{:S(2)}, u32[]{:S(2)}) collective-permute-start(bf16[160,2048]{1,0:T(8,128)(2,1)} %get-tuple-element.41.refs_0_), channel_id=1, source_target_pairs={{0,12},{1,13},{2,14},{3,15},{4,0},{5,1},{6,2},{7,3},{8,4},{9,5},{1... | collective-permute-start | bytes 1966088 | tf_op jit(solution)/shard_map/ppermute | solution.py:378
  10.2 12.4 %collective-permute-start.1 = (bf16[160,2048]{1,0:T(8,128)(2,1)}, bf16[160,2048]{1,0:T(8,128)(2,1)S(1)}, u32[]{:S(2)}, u32[]{:S(2)}) collective-permute-start(bf16[160,2048]{1,0:T(8,128)(2,1)} %get-tuple-element.41.refs_0_), channel_id=1, source_target_pairs={{0,8},{1,9},{2,10},{3,11},{4,12},{5,13},{6,14},{7,15},{8,0},{9,1},... | collective-permute-start | bytes 1966088 | tf_op jit(solution)/shard_map/ppermute | solution.py:378
  13.0 16.6 %collective-permute-start = (bf16[160,2048]{1,0:T(8,128)(2,1)}, bf16[160,2048]{1,0:T(8,128)(2,1)S(1)}, u32[]{:S(2)}, u32[]{:S(2)}) collective-permute-start(bf16[160,2048]{1,0:T(8,128)(2,1)} %get-tuple-element.41.refs_0_), channel_id=1, source_target_pairs={{0,4},{1,5},{2,6},{3,7},{4,8},{5,9},{6,10},{7,11},{8,12},{9,13},{1... | collective-permute-start | bytes 1966088 | tf_op jit(solution)/shard_map/ppermute | solution.py:378
  29.6 1.1 copy-start.1
  35.5 19.0 %collective-permute-start.3 = (bf16[4,80,2048]{2,1,0:T(8,128)(2,1)}, bf16[4,80,2048]{2,1,0:T(8,128)(2,1)S(1)}, u32[]{:S(2)}, u32[]{:S(2)}) collective-permute-start(bf16[4,80,2048]{2,1,0:T(8,128)(2,1)} %get-tuple-element.43), channel_id=1, source_target_pairs={{0,1},{1,2},{2,3},{3,0},{4,5},{5,6},{6,7},{7,4},{8,9},{9,10},{10,1... | collective-permute-start | bytes 3932168 | tf_op jit(solution)/shard_map/ppermute | solution.py:378
  37.1 32.7 %collective-permute-start.4 = (bf16[4,80,2048]{2,1,0:T(8,128)(2,1)}, bf16[4,80,2048]{2,1,0:T(8,128)(2,1)S(1)}, u32[]{:S(2)}, u32[]{:S(2)}) collective-permute-start(bf16[4,80,2048]{2,1,0:T(8,128)(2,1)} %get-tuple-element.44), channel_id=1, source_target_pairs={{0,2},{1,3},{2,0},{3,1},{4,6},{5,7},{6,4},{7,5},{8,10},{9,11},{10,... | collective-permute-start | bytes 3932168 | tf_op jit(solution)/shard_map/ppermute | solution.py:378
  40.0 29.8 %collective-permute-start.5 = (bf16[4,80,2048]{2,1,0:T(8,128)(2,1)}, bf16[4,80,2048]{2,1,0:T(8,128)(2,1)S(1)}, u32[]{:S(2)}, u32[]{:S(2)}) collective-permute-start(bf16[4,80,2048]{2,1,0:T(8,128)(2,1)} %get-tuple-element.45), channel_id=1, source_target_pairs={{0,3},{1,0},{2,1},{3,2},{4,7},{5,4},{6,5},{7,6},{8,11},{9,8},{10,9... | collective-permute-start | bytes 3932168 | tf_op jit(solution)/shard_map/ppermute | solution.py:378
  69.8 1.0 copy-start.4
  69.8 1.5 copy-start.5
  71.3 28.1 %copy-start.2 = (f32[8,2048]{1,0:T(8,128)S(1)}, f32[8,2048]{1,0:T(8,128)}, u32[]{:S(2)}) copy-start(f32[8,2048]{1,0:T(8,128)} %get-tuple-element.47.sum_ref) | copy-start | bytes 196612
  71.3 28.1 %copy-start.3 = (s32[3]{0:T(128)S(1)}, s32[3]{0:T(128)}, u32[]{:S(2)}) copy-start(s32[3]{0:T(128)} %len_ref.3) | copy-start | bytes 40
  85.5 13.8 %all-to-all-start = ((f32[16,48,128]{2,1,0:T(8,128)}), f32[16,48,128]{2,1,0:T(8,128)S(1)}, u32[]{:S(2)}, u32[]{:S(2)}) async-start(f32[16,48,128]{2,1,0:T(8,128)} %get-tuple-element.46), calls=%async_computation | async-start | bytes 786432 | tf_op jit(solution)/shard_map/all_to_all | solution.py:426
  100.7 19.8 %all-to-all-start.1 = ((bf16[16,64,128]{2,1,0:T(8,128)(2,1)}), bf16[16,64,128]{2,1,0:T(8,128)(2,1)S(1)}, u32[]{:S(2)}, u32[]{:S(2)}) async-start(bf16[16,64,128]{2,1,0:T(8,128)(2,1)} %pool.1), calls=%async_computation.1 | async-start | bytes 524288 | tf_op jit(solution)/shard_map/all_to_all | solution.py:437
  109.3 85.8 %all-gather.2.cloned.1.call-start = ((), (), s32[]{:S(2)}) async-start(), calls=%async_computation.3 | async-start | bytes 1253376 | tf_op jit(solution)/shard_map/all_gather | solution.py:425
  142.3 7.4 %copy-start = (bf16[2,768,768]{2,1,0:T(8,128)(2,1)}, bf16[2,768,768]{2,1,0:T(8,128)(2,1)S(1)}, u32[]{:S(2)}) copy-start(bf16[2,768,768]{2,1,0:T(8,128)(2,1)S(1)} %get-tuple-element.68.pre_ref) | copy-start | bytes 7077892
  142.3 3.6 %collective-permute-start.6 = (bf16[1,2,128,768]{3,2,1,0:T(8,128)(2,1)S(1)}, bf16[1,2,128,768]{3,2,1,0:T(8,128)(2,1)S(1)}, u32[]{:S(2)}, u32[]{:S(2)}) collective-permute-start(bf16[1,2,128,768]{3,2,1,0:T(8,128)(2,1)S(1)} %get-tuple-element.56), channel_id=1, source_target_pairs={{0,16},{16,0},{1,17},{17,1},{2,18},{18,2},{3,19},{19,3},{4,20},{20... | collective-permute-start | bytes 1179656 | tf_op jit(solution)/shard_map/ppermute | solution.py:522
  146.1 7.8 %collective-permute-start.7 = (bf16[2,2,128,768]{3,2,1,0:T(8,128)(2,1)S(1)}, bf16[2,2,128,768]{3,2,1,0:T(8,128)(2,1)S(1)}, u32[]{:S(2)}, u32[]{:S(2)}) collective-permute-start(bf16[2,2,128,768]{3,2,1,0:T(8,128)(2,1)S(1)} %get-tuple-element.58), channel_id=1, source_target_pairs={{0,16},{16,0},{1,17},{17,1},{2,18},{18,2},{3,19},{19,3},{4,20},{20... | collective-permute-start | bytes 2359304 | tf_op jit(solution)/shard_map/ppermute | solution.py:522
  146.5 8.2 %collective-permute-start.8 = (bf16[128,768]{1,0:T(8,128)(2,1)S(1)}, bf16[128,768]{1,0:T(8,128)(2,1)S(1)}, u32[]{:S(2)}, u32[]{:S(2)}) collective-permute-start(bf16[128,768]{1,0:T(8,128)(2,1)S(1)} %get-tuple-element.59), channel_id=1, source_target_pairs={{0,32},{32,64},{64,96},{96,128},{128,160},{160,192},{192,224},{224... | collective-permute-start | bytes 589832 | tf_op jit(solution)/shard_map/ppermute | solution.py:525
  146.5 8.2 %collective-permute-start.9 = (bf16[128,768]{1,0:T(8,128)(2,1)S(1)}, bf16[128,768]{1,0:T(8,128)(2,1)S(1)}, u32[]{:S(2)}, u32[]{:S(2)}) collective-permute-start(bf16[128,768]{1,0:T(8,128)(2,1)S(1)} %get-tuple-element.60), channel_id=1, source_target_pairs={{0,224},{32,0},{64,32},{96,64},{128,96},{160,128},{192,160},{224,1... | collective-permute-start | bytes 589832 | tf_op jit(solution)/shard_map/ppermute | solution.py:525
  155.8 13.1 %collective-permute-start.10 = (bf16[2,2,128,768]{3,2,1,0:T(8,128)(2,1)}, bf16[2,2,128,768]{3,2,1,0:T(8,128)(2,1)S(1)}, u32[]{:S(2)}, u32[]{:S(2)}) collective-permute-start(bf16[2,2,128,768]{3,2,1,0:T(8,128)(2,1)} %get-tuple-element.65), channel_id=1, source_target_pairs={{0,16},{16,0},{1,17},{17,1},{2,18},{18,2},{3,19},{19,3},{4,20},{20... | collective-permute-start | bytes 2359304 | tf_op jit(solution)/shard_map/ppermute | solution.py:522
  155.8 12.9 %collective-permute-start.11 = (bf16[2,128,768]{2,1,0:T(8,128)(2,1)}, bf16[2,128,768]{2,1,0:T(8,128)(2,1)S(1)}, u32[]{:S(2)}, u32[]{:S(2)}) collective-permute-start(bf16[2,128,768]{2,1,0:T(8,128)(2,1)} %get-tuple-element.66), channel_id=1, source_target_pairs={{0,32},{32,64},{64,96},{96,128},{128,160},{160,192},{192,224},{224... | collective-permute-start | bytes 1179656 | tf_op jit(solution)/shard_map/ppermute | solution.py:525
  155.8 13.1 %collective-permute-start.12 = (bf16[2,128,768]{2,1,0:T(8,128)(2,1)}, bf16[2,128,768]{2,1,0:T(8,128)(2,1)}, u32[]{:S(2)}, u32[]{:S(2)}) collective-permute-start(bf16[2,128,768]{2,1,0:T(8,128)(2,1)} %get-tuple-element.67), channel_id=1, source_target_pairs={{0,224},{32,0},{64,32},{96,64},{128,96},{160,128},{192,160},{224,1... | collective-permute-start | bytes 1179656 | tf_op jit(solution)/shard_map/ppermute | solution.py:525
  170.2 16.5 %collective-permute-start.13 = (bf16[3,2,128,768]{3,2,1,0:T(8,128)(2,1)S(1)}, bf16[3,2,128,768]{3,2,1,0:T(8,128)(2,1)S(1)}, u32[]{:S(2)}, u32[]{:S(2)}) collective-permute-start(bf16[3,2,128,768]{3,2,1,0:T(8,128)(2,1)S(1)} %get-tuple-element.72), channel_id=1, source_target_pairs={{0,16},{16,0},{1,17},{17,1},{2,18},{18,2},{3,19},{19,3},{4,20},{20... | collective-permute-start | bytes 3538952 | tf_op jit(solution)/shard_map/ppermute | solution.py:522
  170.3 16.4 %collective-permute-start.14 = (bf16[2,128,768]{2,1,0:T(8,128)(2,1)S(1)}, bf16[2,128,768]{2,1,0:T(8,128)(2,1)S(1)}, u32[]{:S(2)}, u32[]{:S(2)}) collective-permute-start(bf16[2,128,768]{2,1,0:T(8,128)(2,1)S(1)} %get-tuple-element.73), channel_id=1, source_target_pairs={{0,32},{32,64},{64,96},{96,128},{128,160},{160,192},{192,224},{224... | collective-permute-start | bytes 1179656 | tf_op jit(solution)/shard_map/ppermute | solution.py:525
  170.4 16.3 %collective-permute-start.15 = (bf16[2,128,768]{2,1,0:T(8,128)(2,1)S(1)}, bf16[2,128,768]{2,1,0:T(8,128)(2,1)S(1)}, u32[]{:S(2)}, u32[]{:S(2)}) collective-permute-start(bf16[2,128,768]{2,1,0:T(8,128)(2,1)S(1)} %get-tuple-element.74), channel_id=1, source_target_pairs={{0,224},{32,0},{64,32},{96,64},{128,96},{160,128},{192,160},{224,1... | collective-permute-start | bytes 1179656 | tf_op jit(solution)/shard_map/ppermute | solution.py:525
  187.8 12.3 %collective-permute-start.16 = (bf16[2,128,768]{2,1,0:T(8,128)(2,1)}, bf16[2,128,768]{2,1,0:T(8,128)(2,1)}, u32[]{:S(2)}, u32[]{:S(2)}) collective-permute-start(bf16[2,128,768]{2,1,0:T(8,128)(2,1)} %get-tuple-element.75), channel_id=1, source_target_pairs={{0,32},{32,64},{64,96},{96,128},{128,160},{160,192},{192,224},{224... | collective-permute-start | bytes 1179656 | tf_op jit(solution)/shard_map/ppermute | solution.py:525
  187.9 12.3 %collective-permute-start.17 = (bf16[2,128,768]{2,1,0:T(8,128)(2,1)}, bf16[2,128,768]{2,1,0:T(8,128)(2,1)}, u32[]{:S(2)}, u32[]{:S(2)}) collective-permute-start(bf16[2,128,768]{2,1,0:T(8,128)(2,1)} %get-tuple-element.76), channel_id=1, source_target_pairs={{0,224},{32,0},{64,32},{96,64},{128,96},{160,128},{192,160},{224,1... | collective-permute-start | bytes 1179656 | tf_op jit(solution)/shard_map/ppermute | solution.py:525
Sparse Core Ops, SparseCore 0:
  159.2 35.8 all-gather.1
